TPU v7x, 512 devices: a whole 4x8x8 slice. The times are simulated.
512 devices in a mesh: section: 16 (over x, z_hi, core), fsdp: 32 (over y, z_lo).
Axes of the slice: x: 4, y: 8, z: 8 (z_hi: 2, z_lo: 4; z = z_hi * 4 + z_lo), core: 2. Of those that a mesh axis runs over, the one named last changes fastest.
Arguments:
- inputs: bfloat16 [4, 32, 32, 2048], P(None, 'fsdp', 'section'), may hold values from -6 to 6
- segments: int32 [4, 32, 32], P(None, 'fsdp', 'section'), may hold values from 0 to 7, never falling along the last dimension, each value on 1 to 16 neighbouring positions
- norm_gains: bfloat16 [16, 2048], P('section', 'fsdp'), may hold values from 0.099609375 to 1.8984375
- w_query: bfloat16 [16, 2048, 1024], P('section', 'fsdp'), may hold values from -0.125 to 0.125
- w_keyval: bfloat16 [16, 2048, 512], P('section', 'fsdp'), may hold values from -0.125 to 0.125
- w_output: bfloat16 [16, 1024, 2048], P('section', 'fsdp'), may hold values from -0.1875 to 0.1875
Outputs:
- hidden: bfloat16 [4, 32, 32, 2048], P(None, 'fsdp', 'section')
Inputs may be any that keep to these rules, and one draw needn't show every extreme that they name: `segments`: within each sequence the numbers never fall, each document spans at most 16 positions, and some document spans exactly that many.
All inputs are finite; a program needn't handle non-finite values.
Results may differ from a plain program's by a relative error of at most 0.034.
Values may be sent and summed in bfloat16 or wider, within the bound.
A program may use at most 64 MiB of HBM per device.

v0:
```python
from functools import partial

import jax
import jax.numpy as jnp
from jax import lax
from jax.sharding import PartitionSpec as P

HEAD = 64
HEADS = 16
KV_HEADS = 4


EPSILON = 1e-05
THETA = 500000.0


def shortened(x):

    def short(part):
        return part.astype(jnp.bfloat16) if part.dtype == jnp.float32 else part

    return jax.tree.map(short, x)


def from_behind(value, axis, steps):
    count = lax.axis_size(axis)
    initial, last = (max(0, -steps), min(count, count - steps))
    return lax.ppermute(value, axis, [(source, source + steps) for source in range(initial, last)])


def rope_tables(seq_len, size):
    position = jnp.arange(seq_len, dtype=jnp.float32)
    freq = THETA ** (-jnp.arange(size // 2, dtype=jnp.float32) * 2.0 / size)
    angle = position[:, None] * freq[None, :]
    return (jnp.cos(angle), jnp.sin(angle))


def rotate(values, cosine, sine_table):
    half_size = values.shape[-1] // 2
    lower_half = values[..., :half_size]
    upper_half = values[..., half_size:]
    cos_part = cosine[:, None, :]
    sin_part = sine_table[:, None, :]
    return jnp.concatenate(
        [
            lower_half * cos_part - upper_half * sin_part,
            upper_half * cos_part + lower_half * sin_part,
        ],
        axis=-1,
    )


def layer_one(rows, segs, gain_row, w_query, w_keyval, w_output):
    seq_len = rows.shape[0]
    hidden_f = rows.astype(jnp.float32)
    scaled = (
        hidden_f
        * lax.rsqrt(jnp.mean(hidden_f * hidden_f, axis=-1, keepdims=True) + EPSILON)
        * gain_row.astype(jnp.float32)
    )
    normed = scaled.astype(jnp.bfloat16)
    queries = jnp.dot(normed, w_query, preferred_element_type=jnp.float32).reshape(
        seq_len, HEADS, HEAD
    )
    keyval = jnp.dot(normed, w_keyval, preferred_element_type=jnp.float32).reshape(
        seq_len, 2, KV_HEADS, HEAD
    )
    cosine, sine_table = rope_tables(seq_len, HEAD)
    queries = rotate(queries, cosine, sine_table).astype(jnp.bfloat16)
    queries = queries.reshape(seq_len, KV_HEADS, HEADS // KV_HEADS, HEAD)
    key_rows = rotate(keyval[:, 0], cosine, sine_table).astype(jnp.bfloat16)
    value_rows = keyval[:, 1].astype(jnp.bfloat16)
    scores = jnp.einsum(
        "skgd,tkd->kgst", queries, key_rows, preferred_element_type=jnp.float32
    ) * HEAD ** (-0.5)
    position = jnp.arange(seq_len)
    allowed = (position[:, None] >= position[None, :]) & (segs[:, None] == segs[None, :])
    exps = jnp.where(allowed[None, None], jnp.exp(scores), 0.0)
    weights_bf = (exps / jnp.sum(exps, axis=-1, keepdims=True)).astype(jnp.bfloat16)
    attended = jnp.einsum(
        "kgst,tkd->skgd", weights_bf, value_rows, preferred_element_type=jnp.float32
    ).astype(jnp.bfloat16)
    update = jnp.dot(
        attended.reshape(seq_len, HEADS * HEAD), w_output, preferred_element_type=jnp.float32
    )
    return (hidden_f + update).astype(jnp.bfloat16)


def shards(inputs, segments, norm_gains, w_query, w_keyval, w_output):
    sections = lax.axis_size("section")
    section_index = lax.axis_index("section")
    micro_count = inputs.shape[0]
    share_len = inputs.shape[2]
    seq_len = share_len * sections
    model_width = inputs.shape[3]
    gathered = (
        lax.all_gather(norm_gains, "fsdp", axis=1, tiled=True),
        lax.all_gather(w_query, "fsdp", axis=1, tiled=True),
        lax.all_gather(w_keyval, "fsdp", axis=1, tiled=True),
        lax.all_gather(w_output, "fsdp", axis=1, tiled=True),
    )
    gain_row = gathered[0][0]
    query_full = gathered[1][0]
    keyval_full = gathered[2][0]
    output_full = gathered[3][0]
    local_rows = inputs[:, 0]
    local_segs = segments[:, 0]

    def fetch_input(step_index):
        which = jnp.minimum(step_index, micro_count - 1)
        own_rows = lax.dynamic_index_in_dim(local_rows, which, 0, keepdims=False)
        own_segs = lax.dynamic_index_in_dim(local_segs, which, 0, keepdims=False)
        fed_rows, fed_segs = (
            lax.all_gather(own_rows, "section", axis=0, tiled=True),
            lax.all_gather(own_segs, "section", axis=0, tiled=True),
        )
        return (fed_rows, fed_segs)

    def deliver(step_index, finished_rows, kept):
        slot_index = step_index - (sections - 1)
        spread_rows = jax.tree.map(
            lambda part, own: part.astype(own.dtype),
            lax.all_to_all(
                shortened(finished_rows), "section", split_axis=0, concat_axis=0, tiled=True
            ),
            finished_rows,
        )
        own_share = spread_rows[(sections - 1) * share_len :]
        kept = lax.dynamic_update_index_in_dim(kept, own_share, slot_index, 0)
        return kept

    def advance(step_index, state_tuple, feeding, finishing):
        previous_rows, previous_segs, kept = state_tuple
        moved_rows, moved_segs = (
            from_behind(shortened(previous_rows), "section", 1).astype(previous_rows.dtype),
            from_behind(shortened(previous_segs), "section", 1).astype(previous_segs.dtype),
        )
        if feeding:
            fed_rows, fed_segs = fetch_input(step_index)
            at_first = section_index == 0
            current_rows = jnp.where(at_first, fed_rows, moved_rows)
            current_segs = jnp.where(at_first, fed_segs, moved_segs)
        else:
            current_rows = moved_rows
            current_segs = moved_segs
        slot_index = step_index - section_index
        active = (slot_index >= 0) & (slot_index < micro_count)

        def run_layer():
            return layer_one(
                current_rows, current_segs, gain_row, query_full, keyval_full, output_full
            )

        def pass_along():
            return current_rows

        output_rows = lax.cond(active, run_layer, pass_along)
        if finishing:
            kept = deliver(step_index, output_rows, kept)
        return (output_rows, current_segs, kept)

    kept_rows = jnp.zeros((micro_count, share_len, model_width), jnp.bfloat16)
    state_tuple = (
        jnp.zeros((seq_len, model_width), jnp.bfloat16),
        jnp.zeros((seq_len,), jnp.int32),
        kept_rows,
    )
    total_steps = micro_count + sections - 1
    marks = sorted(
        set([0, min(micro_count, total_steps), min(sections - 1, total_steps), total_steps])
    )
    for begin_step, end_step in zip(marks[:-1], marks[1:]):
        stepper = partial(
            advance, feeding=begin_step < micro_count, finishing=begin_step >= sections - 1
        )
        state_tuple = lax.fori_loop(begin_step, end_step, stepper, state_tuple)
    kept_rows = state_tuple[2]
    return kept_rows[:, None]


def solution(mesh):
    return jax.shard_map(
        shards,
        mesh=mesh,
        in_specs=(
            P(None, "fsdp", "section", None),
            P(None, "fsdp", "section"),
            P("section", "fsdp"),
            P("section", "fsdp", None),
            P("section", "fsdp", None),
            P("section", "fsdp", None),
        ),
        out_specs=P(None, "fsdp", "section", None),
        check_vma=False,
    )
```

profile of v0, /device:TPU:1, one launch (start us, length us, event | category | flops | bytes accessed | tf_op | source)
XLA Modules:
  0.0 1045.1 jit_solution(9251451146704845298)
XLA Ops:
  13.1 71.4 %all-reduce.1 = bf16[2048]{0:T(1024)(128)(2,1)S(1)} all-reduce(bf16[2048]{0:T(1024)(128)(2,1)S(1)} %dynamic-update-slice.1), channel_id=1, replica_groups=mesh['section'=16,'fsdp'=32] {'fsdp'}, use_global_device_ids=true, to_apply=%add.1 | all-reduce | flops 2048 | bytes 8192 | tf_op jit(solution)/shard_map/squeeze | solution.py:102
  84.5 65.0 %all-gather.9.cloned.1.call-done = bf16[1,2048,512]{2,1,0:T(8,128)(2,1)} async-done(((bf16[1,64,512]{2,1,0:T(8,128)(2,1)}), bf16[1,2048,512]{2,1,0:T(8,128)(2,1)}) %all-gather.9.cloned.1.call-update) | async-done | bytes 2097168 | tf_op jit(solution)/shard_map/all_gather | solution.py:99
  149.5 163.1 %all-gather.11.cloned.1.call-done = bf16[1,2048,1024]{2,1,0:T(8,128)(2,1)} async-done(((bf16[1,64,1024]{2,1,0:T(8,128)(2,1)}), bf16[1,2048,1024]{2,1,0:T(8,128)(2,1)}) %all-gather.11.cloned.1.call-update) | async-done | bytes 4194320 | tf_op jit(solution)/shard_map/all_gather | solution.py:98
  312.6 162.4 %all-gather.13.cloned.1.call-done = bf16[1,1024,2048]{2,1,0:T(8,128)(2,1)} async-done(((bf16[1,32,2048]{2,1,0:T(8,128)(2,1)}), bf16[1,1024,2048]{2,1,0:T(8,128)(2,1)}) %all-gather.13.cloned.1.call-update) | async-done | bytes 4194320 | tf_op jit(solution)/shard_map/all_gather | solution.py:100
  475.1 254.3 %while.55 = (s32[]{:T(128)}, bf16[32,2048]{1,0:T(8,128)(2,1)S(1)}, s32[32]{0:T(128)S(1)}, s32[]{:T(128)}, pred[]{:T(512)}, /*index=5*/bf16[4,2,2048]{2,0,1:T(4,1...) while((s32[]{:T(128)}, bf16[32,2048]{1,0:T(8,128)(2,1)S(1)}, ...), condition=%wide.region_5.6_spmd.clone, body=%wide.region_0.5_spmd.clone.sunk | while | flops 341154528 | bytes 22414952 | solution.py:176
  475.1 27.4 %collective-permute-start.5 = (s32[32]{0:T(128)S(1)}, s32[32]{0:T(128)S(1)}, u32[]{:S(2)}, u32[]{:S(2)}) collective-permute-start(s32[32]{0:T(128)S(1)} %broadcast_select_fusion.4), channel_id=1, source_target_pairs={{0,32},{32,64},{64,96},{96,128},{128,160},{160,192},{192,224},{224... | collective-permute-start | bytes 392 | tf_op jit(solution)/shard_map/while/body/eval_jaxpr/ppermute | solution.py:28
  506.5 12.8 %all-reduce.4 = s32[32]{0:T(128)S(1)} all-reduce(s32[32]{0:T(128)S(1)} %bitcast_dynamic-update-slice_fusion.2), channel_id=3, replica_groups=mesh['section'=16,'fsdp'=32] {'section'}, use_global_device_ids=true, to_apply=%add | all-reduce | flops 32 | bytes 256 | tf_op jit(solution)/shard_map/while/body/eval_jaxpr/all_gather | solution.py:115
  519.4 29.9 %all-gather.4 = bf16[1,32,2048]{2,0,1:T(2,128)(2,1)S(1)} all-gather(bf16[1,2,2048]{2,0,1:T(2,128)(2,1)S(1)} %constant_dynamic-slice_fusion.2), channel_id=2, replica_groups=mesh['section'=16,'fsdp'=32] {'section'}, dimensions={1}, use_global_device_ids=true | all-gather | bytes 139264 | tf_op jit(solution)/shard_map/while/body/eval_jaxpr/all_gather | solution.py:114
  559.3 11.0 %all-reduce.4 = s32[32]{0:T(128)S(1)} all-reduce(s32[32]{0:T(128)S(1)} %bitcast_dynamic-update-slice_fusion.2), channel_id=3, replica_groups=mesh['section'=16,'fsdp'=32] {'section'}, use_global_device_ids=true, to_apply=%add | all-reduce | flops 32 | bytes 256 | tf_op jit(solution)/shard_map/while/body/eval_jaxpr/all_gather | solution.py:115
  570.3 34.8 %all-gather.4 = bf16[1,32,2048]{2,0,1:T(2,128)(2,1)S(1)} all-gather(bf16[1,2,2048]{2,0,1:T(2,128)(2,1)S(1)} %constant_dynamic-slice_fusion.2), channel_id=2, replica_groups=mesh['section'=16,'fsdp'=32] {'section'}, dimensions={1}, use_global_device_ids=true | all-gather | bytes 139264 | tf_op jit(solution)/shard_map/while/body/eval_jaxpr/all_gather | solution.py:114
  627.6 34.2 %all-gather.4 = bf16[1,32,2048]{2,0,1:T(2,128)(2,1)S(1)} all-gather(bf16[1,2,2048]{2,0,1:T(2,128)(2,1)S(1)} %constant_dynamic-slice_fusion.2), channel_id=2, replica_groups=mesh['section'=16,'fsdp'=32] {'section'}, dimensions={1}, use_global_device_ids=true | all-gather | bytes 139264 | tf_op jit(solution)/shard_map/while/body/eval_jaxpr/all_gather | solution.py:114
  661.9 8.6 conditional.9
  686.5 34.2 %all-gather.4 = bf16[1,32,2048]{2,0,1:T(2,128)(2,1)S(1)} all-gather(bf16[1,2,2048]{2,0,1:T(2,128)(2,1)S(1)} %constant_dynamic-slice_fusion.2), channel_id=2, replica_groups=mesh['section'=16,'fsdp'=32] {'section'}, dimensions={1}, use_global_device_ids=true | all-gather | bytes 139264 | tf_op jit(solution)/shard_map/while/body/eval_jaxpr/all_gather | solution.py:114
  720.8 8.6 conditional.9
  729.4 156.7 %while.53 = (s32[]{:T(128)}, bf16[32,2048]{1,0:T(8,128)(2,1)S(1)}, s32[32]{0:T(128)S(1)}, s32[]{:T(128)}, bf16[2048]{0:T(1024)(128)(2,1)S(1)}, /*index=5*/bf16[2...) while((s32[]{:T(128)}, bf16[32,2048]{1,0:T(8,128)(2,1)S(1)}, ...), condition=%wide.region_11.12_spmd, body=%wide.region_6.11_spmd.sunk | while | flops 341088896 | bytes 22126660 | solution.py:176
  756.1 16.3 %collective-permute-start = (bf16[32,2048]{1,0:T(8,128)(2,1)S(1)}, bf16[32,2048]{1,0:T(8,128)(2,1)S(1)}, u32[]{:S(2)}, u32[]{:S(2)}) collective-permute-start(bf16[32,2048]{1,0:T(8,128)(2,1)S(1)} %get-tuple-element.1127), channel_id=1, source_target_pairs={{0,32},{32,64},{64,96},{96,128},{128,160},{160,192},{192,224},{224... | collective-permute-start | bytes 393224 | tf_op jit(solution)/shard_map/while/body/eval_jaxpr/ppermute | solution.py:28
  791.4 8.8 collective-permute-start
  803.2 17.2 %collective-permute-start = (bf16[32,2048]{1,0:T(8,128)(2,1)S(1)}, bf16[32,2048]{1,0:T(8,128)(2,1)S(1)}, u32[]{:S(2)}, u32[]{:S(2)}) collective-permute-start(bf16[32,2048]{1,0:T(8,128)(2,1)S(1)} %get-tuple-element.1127), channel_id=1, source_target_pairs={{0,32},{32,64},{64,96},{96,128},{128,160},{160,192},{192,224},{224... | collective-permute-start | bytes 393224 | tf_op jit(solution)/shard_map/while/body/eval_jaxpr/ppermute | solution.py:28
  836.5 9.1 collective-permute-start
  848.6 9.3 collective-permute-start
  861.0 8.9 collective-permute-start
  874.0 9.1 collective-permute-start
  886.1 152.5 %while.54 = (s32[]{:T(128)}, bf16[32,2048]{1,0:T(8,128)(2,1)S(1)}, s32[32]{0:T(128)S(1)}, bf16[4,2,2048]{2,1,0:T(2,128)(2,1)}, s32[]{:T(128)}, /*index=5*/bf16[2...) while((s32[]{:T(128)}, bf16[32,2048]{1,0:T(8,128)(2,1)S(1)}, ...), condition=%wide.region_17.18_spmd, body=%wide.region_12.17_spmd.sunk | while | flops 341088896 | bytes 22798464 | solution.py:176
  886.1 10.3 collective-permute-start.2
  900.2 31.3 %all-to-all-start = ((bf16[16,2,2048]{2,1,0:T(2,128)(2,1)}), bf16[16,2,2048]{2,1,0:T(2,128)(2,1)S(1)}, u32[]{:S(2)}, u32[]{:S(2)}) async-start(bf16[16,2,2048]{2,1,0:T(2,128)(2,1)} %all_to_all.18), calls=%async_computation | async-start | bytes 262144 | tf_op jit(solution)/shard_map/while/body/eval_jaxpr/all_to_all | solution.py:123
  931.5 10.0 all-to-all-done
  949.6 16.9 %all-to-all-start = ((bf16[16,2,2048]{2,1,0:T(2,128)(2,1)}), bf16[16,2,2048]{2,1,0:T(2,128)(2,1)S(1)}, u32[]{:S(2)}, u32[]{:S(2)}) async-start(bf16[16,2,2048]{2,1,0:T(2,128)(2,1)} %all_to_all.18), calls=%async_computation | async-start | bytes 262144 | tf_op jit(solution)/shard_map/while/body/eval_jaxpr/all_to_all | solution.py:123
  966.6 10.0 all-to-all-done
  983.6 16.7 %all-to-all-start = ((bf16[16,2,2048]{2,1,0:T(2,128)(2,1)}), bf16[16,2,2048]{2,1,0:T(2,128)(2,1)S(1)}, u32[]{:S(2)}, u32[]{:S(2)}) async-start(bf16[16,2,2048]{2,1,0:T(2,128)(2,1)} %all_to_all.18), calls=%async_computation | async-start | bytes 262144 | tf_op jit(solution)/shard_map/while/body/eval_jaxpr/all_to_all | solution.py:123
  1000.4 10.0 all-to-all-done
  1017.4 10.5 %all-to-all-start = ((bf16[16,2,2048]{2,1,0:T(2,128)(2,1)}), bf16[16,2,2048]{2,1,0:T(2,128)(2,1)S(1)}, u32[]{:S(2)}, u32[]{:S(2)}) async-start(bf16[16,2,2048]{2,1,0:T(2,128)(2,1)} %all_to_all.18), calls=%async_computation | async-start | bytes 262144 | tf_op jit(solution)/shard_map/while/body/eval_jaxpr/all_to_all | solution.py:123
  1027.9 10.0 all-to-all-done
  (262 shorter events, 193.8 us)
Async XLA Ops:
  6.5 143.0 %all-gather.9.cloned.1.call-start = ((), (), s32[]{:S(2)}) async-start(), calls=%async_computation.1 | async-start | bytes 2162688 | tf_op jit(solution)/shard_map/all_gather | solution.py:99
  7.3 305.4 %all-gather.11.cloned.1.call-start = ((), (), s32[]{:S(2)}) async-start(), calls=%async_computation.2 | async-start | bytes 4325376 | tf_op jit(solution)/shard_map/all_gather | solution.py:98
  8.0 467.1 %all-gather.13.cloned.1.call-start = ((), (), s32[]{:S(2)}) async-start(), calls=%async_computation.3 | async-start | bytes 4325376 | tf_op jit(solution)/shard_map/all_gather | solution.py:100
  475.1 74.2 %collective-permute-start.5 = (s32[32]{0:T(128)S(1)}, s32[32]{0:T(128)S(1)}, u32[]{:S(2)}, u32[]{:S(2)}) collective-permute-start(s32[32]{0:T(128)S(1)} %broadcast_select_fusion.4), channel_id=1, source_target_pairs={{0,32},{32,64},{64,96},{96,128},{128,160},{160,192},{192,224},{224... | collective-permute-start | bytes 392 | tf_op jit(solution)/shard_map/while/body/eval_jaxpr/ppermute | solution.py:28
  502.5 46.8 %collective-permute-start.4 = (bf16[32,2048]{1,0:T(8,128)(2,1)S(1)}, bf16[32,2048]{1,0:T(8,128)(2,1)S(1)}, u32[]{:S(2)}, u32[]{:S(2)}) collective-permute-start(bf16[32,2048]{1,0:T(8,128)(2,1)S(1)} %get-tuple-element.1080), channel_id=1, source_target_pairs={{0,32},{32,64},{64,96},{96,128},{128,160},{160,192},{192,224},{224... | collective-permute-start | bytes 393224 | tf_op jit(solution)/shard_map/while/body/eval_jaxpr/ppermute | solution.py:28
  549.4 55.6 %collective-permute-start.5 = (s32[32]{0:T(128)S(1)}, s32[32]{0:T(128)S(1)}, u32[]{:S(2)}, u32[]{:S(2)}) collective-permute-start(s32[32]{0:T(128)S(1)} %broadcast_select_fusion.4), channel_id=1, source_target_pairs={{0,32},{32,64},{64,96},{96,128},{128,160},{160,192},{192,224},{224... | collective-permute-start | bytes 392 | tf_op jit(solution)/shard_map/while/body/eval_jaxpr/ppermute | solution.py:28
  555.0 50.1 %collective-permute-start.4 = (bf16[32,2048]{1,0:T(8,128)(2,1)S(1)}, bf16[32,2048]{1,0:T(8,128)(2,1)S(1)}, u32[]{:S(2)}, u32[]{:S(2)}) collective-permute-start(bf16[32,2048]{1,0:T(8,128)(2,1)S(1)} %get-tuple-element.1080), channel_id=1, source_target_pairs={{0,32},{32,64},{64,96},{96,128},{128,160},{160,192},{192,224},{224... | collective-permute-start | bytes 393224 | tf_op jit(solution)/shard_map/while/body/eval_jaxpr/ppermute | solution.py:28
  613.8 48.0 %collective-permute-start.5 = (s32[32]{0:T(128)S(1)}, s32[32]{0:T(128)S(1)}, u32[]{:S(2)}, u32[]{:S(2)}) collective-permute-start(s32[32]{0:T(128)S(1)} %broadcast_select_fusion.4), channel_id=1, source_target_pairs={{0,32},{32,64},{64,96},{96,128},{128,160},{160,192},{192,224},{224... | collective-permute-start | bytes 392 | tf_op jit(solution)/shard_map/while/body/eval_jaxpr/ppermute | solution.py:28
  615.7 46.1 %collective-permute-start.4 = (bf16[32,2048]{1,0:T(8,128)(2,1)S(1)}, bf16[32,2048]{1,0:T(8,128)(2,1)S(1)}, u32[]{:S(2)}, u32[]{:S(2)}) collective-permute-start(bf16[32,2048]{1,0:T(8,128)(2,1)S(1)} %get-tuple-element.1080), channel_id=1, source_target_pairs={{0,32},{32,64},{64,96},{96,128},{128,160},{160,192},{192,224},{224... | collective-permute-start | bytes 393224 | tf_op jit(solution)/shard_map/while/body/eval_jaxpr/ppermute | solution.py:28
  670.5 50.1 %collective-permute-start.5 = (s32[32]{0:T(128)S(1)}, s32[32]{0:T(128)S(1)}, u32[]{:S(2)}, u32[]{:S(2)}) collective-permute-start(s32[32]{0:T(128)S(1)} %broadcast_select_fusion.4), channel_id=1, source_target_pairs={{0,32},{32,64},{64,96},{96,128},{128,160},{160,192},{192,224},{224... | collective-permute-start | bytes 392 | tf_op jit(solution)/shard_map/while/body/eval_jaxpr/ppermute | solution.py:28
  674.7 46.0 %collective-permute-start.4 = (bf16[32,2048]{1,0:T(8,128)(2,1)S(1)}, bf16[32,2048]{1,0:T(8,128)(2,1)S(1)}, u32[]{:S(2)}, u32[]{:S(2)}) collective-permute-start(bf16[32,2048]{1,0:T(8,128)(2,1)S(1)} %get-tuple-element.1080), channel_id=1, source_target_pairs={{0,32},{32,64},{64,96},{96,128},{128,160},{160,192},{192,224},{224... | collective-permute-start | bytes 393224 | tf_op jit(solution)/shard_map/while/body/eval_jaxpr/ppermute | solution.py:28
  729.4 7.0 collective-permute-start
  745.0 11.0 %collective-permute-start = (bf16[32,2048]{1,0:T(8,128)(2,1)S(1)}, bf16[32,2048]{1,0:T(8,128)(2,1)S(1)}, u32[]{:S(2)}, u32[]{:S(2)}) collective-permute-start(bf16[32,2048]{1,0:T(8,128)(2,1)S(1)} %get-tuple-element.1127), channel_id=1, source_target_pairs={{0,32},{32,64},{64,96},{96,128},{128,160},{160,192},{192,224},{224... | collective-permute-start | bytes 393224 | tf_op jit(solution)/shard_map/while/body/eval_jaxpr/ppermute | solution.py:28
  756.1 19.3 %collective-permute-start = (bf16[32,2048]{1,0:T(8,128)(2,1)S(1)}, bf16[32,2048]{1,0:T(8,128)(2,1)S(1)}, u32[]{:S(2)}, u32[]{:S(2)}) collective-permute-start(bf16[32,2048]{1,0:T(8,128)(2,1)S(1)} %get-tuple-element.1127), channel_id=1, source_target_pairs={{0,32},{32,64},{64,96},{96,128},{128,160},{160,192},{192,224},{224... | collective-permute-start | bytes 393224 | tf_op jit(solution)/shard_map/while/body/eval_jaxpr/ppermute | solution.py:28
  775.4 16.0 %collective-permute-start = (bf16[32,2048]{1,0:T(8,128)(2,1)S(1)}, bf16[32,2048]{1,0:T(8,128)(2,1)S(1)}, u32[]{:S(2)}, u32[]{:S(2)}) collective-permute-start(bf16[32,2048]{1,0:T(8,128)(2,1)S(1)} %get-tuple-element.1127), channel_id=1, source_target_pairs={{0,32},{32,64},{64,96},{96,128},{128,160},{160,192},{192,224},{224... | collective-permute-start | bytes 393224 | tf_op jit(solution)/shard_map/while/body/eval_jaxpr/ppermute | solution.py:28
  783.1 8.3 collective-permute-start.1
  791.4 11.8 %collective-permute-start = (bf16[32,2048]{1,0:T(8,128)(2,1)S(1)}, bf16[32,2048]{1,0:T(8,128)(2,1)S(1)}, u32[]{:S(2)}, u32[]{:S(2)}) collective-permute-start(bf16[32,2048]{1,0:T(8,128)(2,1)S(1)} %get-tuple-element.1127), channel_id=1, source_target_pairs={{0,32},{32,64},{64,96},{96,128},{128,160},{160,192},{192,224},{224... | collective-permute-start | bytes 393224 | tf_op jit(solution)/shard_map/while/body/eval_jaxpr/ppermute | solution.py:28
  803.2 20.2 %collective-permute-start = (bf16[32,2048]{1,0:T(8,128)(2,1)S(1)}, bf16[32,2048]{1,0:T(8,128)(2,1)S(1)}, u32[]{:S(2)}, u32[]{:S(2)}) collective-permute-start(bf16[32,2048]{1,0:T(8,128)(2,1)S(1)} %get-tuple-element.1127), channel_id=1, source_target_pairs={{0,32},{32,64},{64,96},{96,128},{128,160},{160,192},{192,224},{224... | collective-permute-start | bytes 393224 | tf_op jit(solution)/shard_map/while/body/eval_jaxpr/ppermute | solution.py:28
  823.4 13.0 %collective-permute-start = (bf16[32,2048]{1,0:T(8,128)(2,1)S(1)}, bf16[32,2048]{1,0:T(8,128)(2,1)S(1)}, u32[]{:S(2)}, u32[]{:S(2)}) collective-permute-start(bf16[32,2048]{1,0:T(8,128)(2,1)S(1)} %get-tuple-element.1127), channel_id=1, source_target_pairs={{0,32},{32,64},{64,96},{96,128},{128,160},{160,192},{192,224},{224... | collective-permute-start | bytes 393224 | tf_op jit(solution)/shard_map/while/body/eval_jaxpr/ppermute | solution.py:28
  832.0 4.5 collective-permute-start.1
  836.5 12.1 %collective-permute-start = (bf16[32,2048]{1,0:T(8,128)(2,1)S(1)}, bf16[32,2048]{1,0:T(8,128)(2,1)S(1)}, u32[]{:S(2)}, u32[]{:S(2)}) collective-permute-start(bf16[32,2048]{1,0:T(8,128)(2,1)S(1)} %get-tuple-element.1127), channel_id=1, source_target_pairs={{0,32},{32,64},{64,96},{96,128},{128,160},{160,192},{192,224},{224... | collective-permute-start | bytes 393224 | tf_op jit(solution)/shard_map/while/body/eval_jaxpr/ppermute | solution.py:28
  848.6 12.3 %collective-permute-start = (bf16[32,2048]{1,0:T(8,128)(2,1)S(1)}, bf16[32,2048]{1,0:T(8,128)(2,1)S(1)}, u32[]{:S(2)}, u32[]{:S(2)}) collective-permute-start(bf16[32,2048]{1,0:T(8,128)(2,1)S(1)} %get-tuple-element.1127), channel_id=1, source_target_pairs={{0,32},{32,64},{64,96},{96,128},{128,160},{160,192},{192,224},{224... | collective-permute-start | bytes 393224 | tf_op jit(solution)/shard_map/while/body/eval_jaxpr/ppermute | solution.py:28
  861.0 12.9 %collective-permute-start = (bf16[32,2048]{1,0:T(8,128)(2,1)S(1)}, bf16[32,2048]{1,0:T(8,128)(2,1)S(1)}, u32[]{:S(2)}, u32[]{:S(2)}) collective-permute-start(bf16[32,2048]{1,0:T(8,128)(2,1)S(1)} %get-tuple-element.1127), channel_id=1, source_target_pairs={{0,32},{32,64},{64,96},{96,128},{128,160},{160,192},{192,224},{224... | collective-permute-start | bytes 393224 | tf_op jit(solution)/shard_map/while/body/eval_jaxpr/ppermute | solution.py:28
  874.0 12.1 %collective-permute-start = (bf16[32,2048]{1,0:T(8,128)(2,1)S(1)}, bf16[32,2048]{1,0:T(8,128)(2,1)S(1)}, u32[]{:S(2)}, u32[]{:S(2)}) collective-permute-start(bf16[32,2048]{1,0:T(8,128)(2,1)S(1)} %get-tuple-element.1127), channel_id=1, source_target_pairs={{0,32},{32,64},{64,96},{96,128},{128,160},{160,192},{192,224},{224... | collective-permute-start | bytes 393224 | tf_op jit(solution)/shard_map/while/body/eval_jaxpr/ppermute | solution.py:28
  886.1 13.3 %collective-permute-start.2 = (bf16[32,2048]{1,0:T(8,128)(2,1)S(1)}, bf16[32,2048]{1,0:T(8,128)(2,1)S(1)}, u32[]{:S(2)}, u32[]{:S(2)}) collective-permute-start(bf16[32,2048]{1,0:T(8,128)(2,1)S(1)} %get-tuple-element.1162), channel_id=1, source_target_pairs={{0,32},{32,64},{64,96},{96,128},{128,160},{160,192},{192,224},{224... | collective-permute-start | bytes 393224 | tf_op jit(solution)/shard_map/while/body/eval_jaxpr/ppermute | solution.py:28
  900.2 41.3 %all-to-all-start = ((bf16[16,2,2048]{2,1,0:T(2,128)(2,1)}), bf16[16,2,2048]{2,1,0:T(2,128)(2,1)S(1)}, u32[]{:S(2)}, u32[]{:S(2)}) async-start(bf16[16,2,2048]{2,1,0:T(2,128)(2,1)} %all_to_all.18), calls=%async_computation | async-start | bytes 262144 | tf_op jit(solution)/shard_map/while/body/eval_jaxpr/all_to_all | solution.py:123
  942.1 6.8 collective-permute-start.2
  949.6 26.9 %all-to-all-start = ((bf16[16,2,2048]{2,1,0:T(2,128)(2,1)}), bf16[16,2,2048]{2,1,0:T(2,128)(2,1)S(1)}, u32[]{:S(2)}, u32[]{:S(2)}) async-start(bf16[16,2,2048]{2,1,0:T(2,128)(2,1)} %all_to_all.18), calls=%async_computation | async-start | bytes 262144 | tf_op jit(solution)/shard_map/while/body/eval_jaxpr/all_to_all | solution.py:123
  977.2 5.7 collective-permute-start.2
  983.6 26.8 %all-to-all-start = ((bf16[16,2,2048]{2,1,0:T(2,128)(2,1)}), bf16[16,2,2048]{2,1,0:T(2,128)(2,1)S(1)}, u32[]{:S(2)}, u32[]{:S(2)}) async-start(bf16[16,2,2048]{2,1,0:T(2,128)(2,1)} %all_to_all.18), calls=%async_computation | async-start | bytes 262144 | tf_op jit(solution)/shard_map/while/body/eval_jaxpr/all_to_all | solution.py:123
  1011.0 5.6 collective-permute-start.2
  1017.4 20.5 %all-to-all-start = ((bf16[16,2,2048]{2,1,0:T(2,128)(2,1)}), bf16[16,2,2048]{2,1,0:T(2,128)(2,1)S(1)}, u32[]{:S(2)}, u32[]{:S(2)}) async-start(bf16[16,2,2048]{2,1,0:T(2,128)(2,1)} %all_to_all.18), calls=%async_computation | async-start | bytes 262144 | tf_op jit(solution)/shard_map/while/body/eval_jaxpr/all_to_all | solution.py:123
  (17 other events, 53.7 us)
Sparse Core Ops, SparseCore 0:
  9.4 140.0 all-gather.8
  151.6 160.9 all-gather.10
  314.7 160.3 all-gather.12
where the time goes:
time: 1050 us
  waiting for transfers between devices  445 us (42%)
  starting transfers between devices  289 us (28%)
  blocking collectives  244 us (23%)
  matrix products  29.3 us (3%)
  local copies, waits for them, and re-layouts  17.2 us (2%)
  between operations  13.8 us (1%)
    ppermute x38, starting transfers between devices, from_behind(): lax.ppermute(value, axis, [(source, source + steps) for source in range(i...  213 us
    all_gather x1, waiting for transfers between devices, shards(): lax.all_gather(w_query, 'fsdp', axis=1, tiled=True)  163 us
    all_gather x1, waiting for transfers between devices, shards(): lax.all_gather(w_output, 'fsdp', axis=1, tiled=True)  162 us
    all_gather x4, blocking collectives, fetch_input(): lax.all_gather(own_rows, 'section', axis=0, tiled=True)  133 us
    all_to_all x4, starting transfers between devices, deliver(): lax.all_to_all(shortened(finished_rows), 'section', split_axis=0, concat_...  75.4 us
    squeeze x1, blocking collectives, shards(): gain_row = gathered[0][0]  71.4 us
    all_gather x1, waiting for transfers between devices, shards(): lax.all_gather(w_keyval, 'fsdp', axis=1, tiled=True)  65 us
    all_to_all x4, waiting for transfers between devices, deliver(): lax.all_to_all(shortened(finished_rows), 'section', split_axis=0, concat_...  40.1 us
  transfers between devices with their start and end apart: 45, of which 22 were waited for; matrix products, arithmetic and copies ran while one was open for 1% of the time, Pallas kernels for 0%

commit v1 on v0

v1 whole, which is shorter than its diff:
```python
import jax
import jax.numpy as jnp
import numpy as np
from jax import lax
from jax.experimental import pallas as pl
from jax.experimental.pallas import tpu as pltpu
from jax.sharding import PartitionSpec as P

MESH = pl.DeviceIdType.MESH
BF16 = jnp.bfloat16
F32 = jnp.float32
EPSILON = 1e-05
THETA = 500000.0
SEQ = 32
MICRO = 4
WIDTH = 2048
CHUNKS = 4
CHUNK = WIDTH // CHUNKS
QW = 1024
KW = 256
QKV = 1536
LAST = 15


def rope_tables():
    position = np.arange(SEQ, dtype=np.float32)
    freq = (THETA ** (-np.arange(32, dtype=np.float32) * 2.0 / 64)).astype(np.float32)
    angle = (position[:, None] * freq[None, :]).astype(np.float32)
    c, s = np.cos(angle), np.sin(angle)
    return (
        np.concatenate([c, c, c, c], 1).astype(np.float32),
        np.concatenate([-s, s, -s, s], 1).astype(np.float32),
    )


def attention(acc, squares, cosine, sine, mask_t):
    acc = acc * lax.rsqrt(squares * (1.0 / WIDTH) + EPSILON)
    width = QW + KW
    qk = acc[:, :width]
    lane = lax.broadcasted_iota(jnp.int32, (SEQ, width), 1)
    swapped = jnp.where(
        (lane & 63) < 32, pltpu.roll(qk, width - 32, 1), pltpu.roll(qk, 32, 1)
    )
    tiles = width // 128
    qk = (
        qk * jnp.concatenate([cosine] * tiles, axis=1)
        + swapped * jnp.concatenate([sine] * tiles, axis=1)
    ).astype(BF16)
    values = acc[:, width:].astype(BF16)
    outs = []
    for g in range(4):
        key = qk[:, QW + 64 * g : QW + 64 * g + 64]
        value = values[:, 64 * g : 64 * g + 64]
        queries = jnp.concatenate(
            [qk[:, 256 * g + 64 * i : 256 * g + 64 * i + 64] for i in range(4)], axis=0
        )
        scores = lax.dot_general(
            key, queries, (((1,), (1,)), ((), ())), preferred_element_type=F32
        )
        scores = jnp.where(mask_t, scores * 0.125, -1e30)
        exps = jnp.exp(scores - jnp.max(scores, axis=0, keepdims=True))
        probs = (exps / jnp.sum(exps, axis=0, keepdims=True)).astype(BF16)
        mixed = lax.dot_general(
            probs, value, (((0,), (0,)), ((), ())), preferred_element_type=F32
        )
        outs.append(jnp.concatenate([mixed[32 * i : 32 * i + 32] for i in range(4)], axis=1))
    return jnp.concatenate(outs, axis=1).astype(BF16)


def kernel(
    in_ref, wa_ref, wb_ref, cos_ref, sin_ref, out_ref,
    w1, w2, xin, mask, xrecv, xsend, staged, owned,
    z_send, z_recv, ring_send, ring_recv, sib_send, sib_recv,
    in_send, in_recv, mask_send, mask_recv, x_send, x_recv, o_send, o_recv,
):
    section, fsdp = lax.axis_index("section"), lax.axis_index("fsdp")
    x, zhi, core = section // 4, (section // 2) % 2, section % 2
    y, z = fsdp // 4, fsdp % 4
    half = ((z + 1) // 2) % 2
    layer = (2 * x + zhi) * 2 + half
    plane = section - core

    def remote(src, dst, send, recv, to_section, to_fsdp):
        return pltpu.make_async_remote_copy(
            src_ref=src, dst_ref=dst, send_sem=send, recv_sem=recv,
            device_id=(to_section, to_fsdp), device_id_type=MESH,
        )

    def arrived(dst, recv):
        remote(dst, dst, z_send.at[0], recv, plane + 1 - core, fsdp).wait_recv()

    own_positions = xin.at[:, pl.ds(2 * section, 2)]
    in_section, in_fsdp = z % 2, y * 4 + 3 * (z // 2)
    in_self = (section == in_section) & (fsdp == in_fsdp)
    in_remote = remote(in_ref, own_positions, in_send, in_recv, in_section, in_fsdp)
    in_local = pltpu.make_async_copy(in_ref, own_positions, in_recv)

    @pl.when(in_self)
    def _():
        in_local.start()

    @pl.when(jnp.logical_not(in_self))
    def _():
        in_remote.start()

    pair, odd = z // 2, z % 2
    z_copies = []
    for part, (src, full, rows) in enumerate(((wa_ref, w1, 64), (wb_ref, w2, 32))):
        for t in range(2):
            to_z = core if t == 0 else 3 - core
            dst = full.at[y, pair, pl.ds(pl.multiple_of(odd * rows, rows), rows)]
            is_self = (pair == core) & (to_z == z)
            far = remote(
                src, dst, z_send.at[part * 2 + t], z_recv.at[part * 2 + odd],
                plane + pair, y * 4 + to_z,
            )
            near = pltpu.make_async_copy(src, dst, z_recv.at[part * 2 + odd])

            @pl.when(is_self)
            def _(near=near):
                near.start()

            @pl.when(jnp.logical_not(is_self))
            def _(far=far):
                far.start()

            z_copies.append((is_self, far))

    right, left = ((y + 1) % 8) * 4 + z, ((y + 7) % 8) * 4 + z
    sibling = plane + 1 - core
    sends = []
    counts = [0, 0]

    def ring(full, column, rows, direction, step, part):
        ref = full.at[column, core, rows]
        copy = remote(
            ref, ref, ring_send.at[counts[0]], ring_recv.at[(direction * 4 + step) * 2 + part],
            section, right if direction == 0 else left,
        )
        counts[0] += 1
        copy.start()
        sends.append(copy)

    def across(full, column, rows, part):
        ref = full.at[column, core, rows]
        copy = remote(ref, ref, sib_send.at[counts[1]], sib_recv.at[part], sibling, fsdp)
        counts[1] += 1
        copy.start()
        sends.append(copy)

    sizes = ((w1, 64), (w2, 32))
    for part, (full, rows) in enumerate(sizes):
        for u in range(2):
            arrived(full.at[y, core, pl.ds(u * rows, rows)], z_recv.at[part * 2 + u])
        whole = pl.ds(0, 2 * rows)
        for direction in range(2):
            ring(full, y, whole, direction, 0, part)
        across(full, y, whole, part)
    for step in range(1, 5):
        for part, (full, rows) in enumerate(sizes):
            for direction in range(2):
                column = (y + (8 - step if direction == 0 else step)) % 8
                kept = pl.ds(direction * rows, rows)
                whole = pl.ds(0, 2 * rows)
                got = whole if step < 4 else kept
                arrived(
                    full.at[column, core, got],
                    ring_recv.at[(direction * 4 + step - 1) * 2 + part],
                )
                if step < 4:
                    ring(full, column, whole if step < 3 else kept, direction, step, part)
                across(full, column, got, part)
    for part, (full, rows) in enumerate(sizes):
        arrived(full.at[:, 1 - core], sib_recv.at[part])

    first = layer == 0
    last = layer == LAST

    @pl.when(first)
    def _():
        arrived(xin, in_recv)
        row = lax.broadcasted_iota(jnp.int32, (SEQ, 128), 0)
        query = lax.broadcasted_iota(jnp.int32, (SEQ, 128), 1) % SEQ

        def load(m, carry):
            for i in range(16):
                xrecv[m, i // 4, :, (i % 4) * 128 : (i % 4) * 128 + 128] = xin[m, :, i, :].astype(BF16)
            seg = xin[m, :, 16, :]
            of_query = jnp.sum(jnp.where(row == query, seg, 0.0), axis=0, keepdims=True)
            allowed = (query >= row) & (seg == of_query)
            mask[m] = jnp.where(allowed, 1.0, 0.0).astype(BF16)
            return carry

        lax.fori_loop(0, MICRO, load, 0)

    @pl.when(jnp.logical_not(first))
    def _():
        arrived(mask, mask_recv)

    next_z = jnp.where(half == 0, jnp.where(z == 0, 2, 1), jnp.where(z == 2, 0, 3))
    next_zhi = jnp.where(half == 0, zhi, 1 - zhi)
    next_x = jnp.where((half == 1) & (zhi == 1), x + 1, x)
    next_section, next_fsdp = next_x * 4 + next_zhi * 2 + core, y * 4 + next_z
    mask_copy = remote(mask, mask, mask_send, mask_recv, next_section, next_fsdp)

    @pl.when(jnp.logical_not(last))
    def _():
        mask_copy.start()

    def hop(m, j):
        return remote(
            xsend.at[m, j], xrecv.at[m, j], x_send.at[m * CHUNKS + j],
            x_recv.at[m * CHUNKS + j], next_section, next_fsdp,
        )

    owner_fsdp = y * 4 + jnp.where(z == 2, 0, 2) + core

    def delivery(m, s):
        return remote(
            staged.at[m, pl.ds(2 * s, 2)], owned.at[m], o_send.at[m * 16 + s], o_recv,
            s, owner_fsdp,
        )

    def one(m, carry):
        acc = jnp.zeros((SEQ, QKV), F32)
        squares = jnp.zeros((SEQ, 1), F32)
        for j in range(CHUNKS):
            @pl.when(jnp.logical_not(first))
            def _(j=j):
                arrived(xrecv.at[m, j], x_recv.at[m * CHUNKS + j])

            h = xrecv[m, j]
            hf = h.astype(F32)
            squares = squares + jnp.sum(hf * hf, axis=1, keepdims=True)
            acc = acc + jnp.dot(
                h, w1[2 * j : 2 * j + 2].reshape(CHUNK, QKV), preferred_element_type=F32
            )
        attended = attention(
            acc, squares, cos_ref[...], sin_ref[...], mask[m].astype(F32) > 0.5
        )
        for j in range(CHUNKS):
            update = jnp.dot(
                attended, w2[:, :, :, j * CHUNK : (j + 1) * CHUNK].reshape(QW, CHUNK),
                preferred_element_type=F32,
            )
            h = xrecv[m, j].astype(F32) + update

            @pl.when(jnp.logical_not(last))
            def _(j=j, h=h):
                xsend[m, j] = h.astype(BF16)
                hop(m, j).start()

            @pl.when(last)
            def _(j=j, h=h):
                for i in range(4):
                    staged[m, :, 4 * j + i, :] = h[:, 128 * i : 128 * i + 128]

        @pl.when(last)
        def _():
            def give(s, carry):
                delivery(m, s).start()
                return carry

            lax.fori_loop(0, 16, give, 0)

        return carry

    lax.fori_loop(0, MICRO, one, 0)

    arrived(owned, o_recv)
    out_ref[...] = owned[...]

    @pl.when(jnp.logical_not(in_self))
    def _():
        in_remote.wait_send()

    for is_self, far in z_copies:
        @pl.when(jnp.logical_not(is_self))
        def _(far=far):
            far.wait_send()

    for copy in sends:
        copy.wait_send()

    @pl.when(jnp.logical_not(last))
    def _():
        mask_copy.wait_send()

        def drain(n, carry):
            hop(n // CHUNKS, n % CHUNKS).wait_send()
            return carry

        lax.fori_loop(0, MICRO * CHUNKS, drain, 0)

    @pl.when(last)
    def _():
        def drain(n, carry):
            delivery(n // 16, n % 16).wait_send()
            return carry

        lax.fori_loop(0, MICRO * 16, drain, 0)


def shards(inputs, segments, norm_gains, w_query, w_keyval, w_output):
    rows = inputs[:, 0].astype(F32).reshape(MICRO, 2, 16, 128)
    segs = jnp.broadcast_to(segments[:, 0].astype(F32)[:, :, None, None], (MICRO, 2, 8, 128))
    positions = jnp.concatenate([rows, segs], axis=2)
    gains = norm_gains[0].astype(F32)[:, None]
    wa = jnp.concatenate([w_query[0], w_keyval[0]], axis=1).astype(F32) * gains
    cosine, sine = rope_tables()
    vmem = pl.BlockSpec(memory_space=pltpu.VMEM)
    hbm = pl.BlockSpec(memory_space=pl.ANY)
    dma = pltpu.SemaphoreType.DMA
    out = pl.pallas_call(
        kernel,
        out_shape=jax.ShapeDtypeStruct((MICRO, 2, 16, 128), F32),
        in_specs=[hbm, hbm, hbm, vmem, vmem],
        out_specs=vmem,
        scratch_shapes=[
            pltpu.VMEM((8, 2, 128, QKV), BF16),
            pltpu.VMEM((8, 2, 64, WIDTH), BF16),
            pltpu.VMEM((MICRO, SEQ, 24, 128), F32),
            pltpu.VMEM((MICRO, SEQ, 128), BF16),
            pltpu.VMEM((MICRO, CHUNKS, SEQ, CHUNK), BF16),
            pltpu.VMEM((MICRO, CHUNKS, SEQ, CHUNK), BF16),
            pltpu.VMEM((MICRO, SEQ, 16, 128), F32),
            pltpu.VMEM((MICRO, 2, 16, 128), F32),
            dma((4,)), dma((4,)), dma((16,)), dma((16,)), dma((18,)), dma((2,)),
            dma, dma, dma, dma, dma((16,)), dma((16,)), dma((64,)), dma,
        ],
        compiler_params=pltpu.CompilerParams(
            has_side_effects=True, vmem_limit_bytes=40 * 1024 * 1024
        ),
        name="stack",
    )(positions, wa.astype(BF16), w_output[0], jnp.asarray(cosine), jnp.asarray(sine))
    return out.astype(BF16).reshape(MICRO, 1, 2, WIDTH)


def solution(mesh):
    return jax.shard_map(
        shards,
        mesh=mesh,
        in_specs=(
            P(None, "fsdp", "section", None),
            P(None, "fsdp", "section"),
            P("section", "fsdp"),
            P("section", "fsdp", None),
            P("section", "fsdp", None),
            P("section", "fsdp", None),
        ),
        out_specs=P(None, "fsdp", "section", None),
        check_vma=False,
    )
```

time: 1050 us -> 218 us (0.21)
  waiting for transfers between devices: 445 us -> 0 us
  starting transfers between devices: 289 us -> 0 us
  blocking collectives: 244 us -> 0 us
  Pallas kernels: 0 us -> 214 us
  matrix products: 29.3 us -> 0 us
  local copies, waits for them, and re-layouts: 17.2 us -> 2.48 us
  between operations: 13.8 us -> 0.05 us
    all_gather x3 -> x0, waiting for transfers between devices: 391 us -> none  [the longest x1 163 us: shards(): lax.all_gather(w_query, 'fsdp', axis=1, tiled=True)]
    pallas_call x0 -> x1, Pallas kernels: none -> 214 us  [shards(): pl.pallas_call(kernel, out_shape=jax.ShapeDtypeStruct((MICRO, 2, 16, 128)...]
    ppermute x38 -> x0, starting transfers between devices: 213 us -> none  [from_behind(): lax.ppermute(value, axis, [(source, source + steps) for source in range(i...]
    all_gather x8 -> x0, blocking collectives: 173 us -> none  [the longest x4 133 us: fetch_input(): lax.all_gather(own_rows, 'section', axis=0, tiled=True)]
    all_to_all x4 -> x0, starting transfers between devices: 75.4 us -> none  [deliver(): lax.all_to_all(shortened(finished_rows), 'section', split_axis=0, concat_...]
    squeeze x1 -> x0, blocking collectives: 71.4 us -> none  [shards(): gain_row = gathered[0][0]]
    all_to_all x4 -> x0, waiting for transfers between devices: 40.1 us -> none  [deliver(): lax.all_to_all(shortened(finished_rows), 'section', split_axis=0, concat_...]
    dot_general x20 -> x0, matrix products: 29.3 us -> none  [the longest x4 12.7 us: layer_one(): jnp.dot(normed, w_query, preferred_element_type=jnp.float32)]
  transfers between devices with their start and end apart: 45 -> 0, of which waited for: 22 -> 0; matrix products, arithmetic and copies ran while one was open for 1% -> 0% of each run, Pallas kernels for 0% -> 0%
where the time goes in v1:
time: 218 us
  Pallas kernels  214 us (98%)
  local copies, waits for them, and re-layouts  2.48 us (1%)
    pallas_call x1, Pallas kernels, shards(): pl.pallas_call(kernel, out_shape=jax.ShapeDtypeStruct((MICRO, 2, 16, 128)...  214 us

profile of v1, /device:TPU:1, one launch (start us, length us, event | category | flops | bytes accessed | tf_op | source)
XLA Modules:
  0.0 217.9 jit_solution(10194629709267900869)
XLA Ops:
  0.0 0.0 copy-start.5
  0.0 0.7 bitcast_convert_fusion
  0.7 0.7 convert_bitcast_fusion
  1.3 0.1 copy.9
  1.4 0.1 broadcast_in_dim.2
  1.5 0.0 copy-done.5
  1.5 0.0 copy-start.3
  1.6 0.0 copy-start.4
  1.6 0.9 copy-done.3
  2.4 0.0 copy-done.4
  2.4 0.0 copy-start
  2.4 0.0 copy-start.1
  2.4 0.0 copy-start.2
  2.4 0.1 multiply_convert_fusion.wa_ref
  2.5 0.8 copy-done
  3.3 0.0 copy-done.1
  3.3 0.0 copy-done.2
  3.3 213.9 %stack.1 = f32[4,2,16,128]{3,2,1,0:T(8,128)S(1)} custom-call(f32[4,2,24,128]{3,2,1,0:T(8,128)S(1)} %pad_maximum_fusion.in_ref, bf16[64,1536]{1,0:T(8,128)(2,1)S(1)} %multiply_convert_fusion.wa_ref, bf16[32,2048]{1,0:T(8,128)(2,1)S(1)} %bitcast.11, f32[32,128]{1,0:T(8,128)S(1)} %copy-done.2, f32[32,128]{1,0:T(8,128)S(1)} %copy-done.1), custom_call_target="tpu_custom_call" | custom-call | tf_op jit(solution)/shard_map/stack/pallas_call | solution.py:314
  217.3 0.6 reshape.20
  (3 shorter events, 0.0 us)
Async XLA Ops:
  0.0 1.5 copy-start.5
  1.5 0.9 copy-start.3
  1.6 0.9 copy-start.4
  2.4 0.9 copy-start
  2.4 0.9 copy-start.1
  2.4 0.9 copy-start.2

commit v2 on v1

v2 whole, which is shorter than its diff:
```python
import jax
import jax.numpy as jnp
import numpy as np
from jax import lax
from jax.experimental import pallas as pl
from jax.experimental.pallas import tpu as pltpu
from jax.sharding import PartitionSpec as P

MESH = pl.DeviceIdType.MESH
BF16 = jnp.bfloat16
F32 = jnp.float32
EPSILON = 1e-05
THETA = 500000.0
SEQ = 32
MICRO = 4
WIDTH = 2048
CHUNKS = 4
CHUNK = WIDTH // CHUNKS
QW = 1024
KW = 256
QKV = 1536
LAST = 15


def rope_tables():
    position = np.arange(SEQ, dtype=np.float32)
    freq = (THETA ** (-np.arange(32, dtype=np.float32) * 2.0 / 64)).astype(np.float32)
    angle = (position[:, None] * freq[None, :]).astype(np.float32)
    c, s = np.cos(angle), np.sin(angle)
    return (
        np.concatenate([c, c, c, c], 1).astype(np.float32),
        np.concatenate([-s, s, -s, s], 1).astype(np.float32),
    )


def attention(accs, squares, cosine, sine, mask):
    scale = lax.rsqrt(squares * (1.0 / WIDTH) + EPSILON)
    cosine, sine = cosine * scale, sine * scale
    lane = lax.broadcasted_iota(jnp.int32, (SEQ, 128), 1)
    low, left = (lane & 63) < 32, lane < 64

    def rope(tile):
        swapped = jnp.where(low, pltpu.roll(tile, 96, 1), pltpu.roll(tile, 32, 1))
        return tile * cosine + swapped * sine

    zero = jnp.zeros((SEQ, 128), F32)
    block = lax.broadcasted_iota(jnp.int32, (64, 128), 1) // SEQ
    keys, values = [], []
    for i in range(2):
        key = rope(accs[4][:, 128 * i : 128 * i + 128])
        keys.append(jnp.transpose(jnp.concatenate([key] * 4, axis=0)))
        value = accs[5][:, 128 * i : 128 * i + 128] * scale
        other = pltpu.roll(value, 64, 1)
        for a, b in ((value, other), (other, value)):
            halves = [jnp.where(left, a, zero), jnp.where(left, zero, b)]
            values.append(jnp.concatenate(halves * 2, axis=0).astype(BF16))
    exps = []
    for g in range(4):
        key = keys[g // 2][64 * (g % 2) : 64 * (g % 2) + 64]
        spread = jnp.concatenate([jnp.where(block == h, key, 0.0) for h in range(4)], axis=0)
        query = jnp.concatenate(
            [rope(accs[g][:, 128 * i : 128 * i + 128]) for i in range(2)], axis=1
        )
        scores = jnp.dot(query.astype(BF16), spread.astype(BF16), preferred_element_type=F32)
        exps.append(jnp.where(mask, jnp.exp(scores * 0.125), 0.0))
    exps = jnp.concatenate(exps, axis=0)
    most = (exps * 0.99609375).astype(BF16)
    rest = (exps - most.astype(F32)).astype(BF16)
    row = lax.broadcasted_iota(jnp.int32, (128, 128), 0) // SEQ
    col = lax.broadcasted_iota(jnp.int32, (128, 128), 1) // SEQ
    same = jnp.where(row == col, 1.0, 0.0).astype(BF16)
    total = jnp.dot(most, same, preferred_element_type=F32) + jnp.dot(
        rest, same, preferred_element_type=F32
    )
    power = jnp.where(total > 1.0, 2.0**-8, 2.0**8)
    probs = (exps * power) * (1.0 / (total * power))
    outs = []
    for g in range(4):
        part = probs[SEQ * g : SEQ * g + SEQ]
        part = jnp.concatenate([jnp.where(left, part, 0.0), jnp.where(left, 0.0, part)], axis=0)
        mixed = jnp.dot(part.astype(BF16), values[g], preferred_element_type=F32).astype(BF16)
        outs += [mixed[:SEQ], mixed[SEQ:]]
    return jnp.concatenate(outs, axis=1)


def kernel(
    in_ref, seg_ref, wa_ref, wb_ref, cos_ref, sin_ref, out_ref,
    w1, w2, xin, segs, wide, mask, xrecv, xsend, staged, owned,
    z_send, z_recv, ring_send, ring_recv, sib_send, sib_recv, cross_send, cross_recv,
    in_send, in_recv, mask_send, mask_recv, x_send, x_recv, o_send, o_recv,
):
    section, fsdp = lax.axis_index("section"), lax.axis_index("fsdp")
    x, zhi, core = section // 4, (section // 2) % 2, section % 2
    y, zlo = fsdp // 4, fsdp % 4
    z = zhi * 4 + zlo
    side = ((x + 1) // 2) % 2
    layer = jnp.where(x < 2, (z + 6) % 8, 8 + (9 - z) % 8)
    first, last = layer == 0, layer == LAST
    plane = section - core

    def place(at_x, at_z, at_core):
        return at_x * 4 + (at_z // 4) * 2 + at_core, y * 4 + at_z % 4

    def host(of_layer, of_side, at_core):
        early = of_layer < 8
        at_x = jnp.where(early, of_side, 3 - of_side)
        return place(at_x, jnp.where(early, of_layer + 2, 17 - of_layer) % 8, at_core)

    def remote(src, dst, send, recv, to):
        return pltpu.make_async_remote_copy(
            src_ref=src, dst_ref=dst, send_sem=send, recv_sem=recv,
            device_id=to, device_id_type=MESH,
        )

    def is_me(to):
        return (to[0] == section) & (to[1] == fsdp)

    sibling = (plane + 1 - core, fsdp)
    partner = place(jnp.where(x < 2, 1 - x, 5 - x), z, core)
    right = (section, ((y + 1) % 8) * 4 + zlo)
    left = (section, ((y + 7) % 8) * 4 + zlo)

    def arrived(dst, recv):
        remote(dst, dst, z_send.at[0], recv, sibling).wait_recv()

    in_to = host(jnp.int32(0), zlo // 2, zlo % 2)
    own_layer = section
    a_to = host(own_layer, zlo // 2, zlo % 2)
    b_to = [host(own_layer, q, zlo // 2) for q in range(2)]
    next_to = host(jnp.minimum(layer + 1, LAST), side, core)
    prev_from = host(jnp.maximum(layer - 1, 0), side, core)
    owner_fsdp = y * 4 + 2 * side + core
    result_from = host(jnp.int32(LAST), zlo // 2, zlo % 2)
    a_from = (layer, y * 4 + 2 * side + core)
    b_from = [(layer, y * 4 + 2 * core + u) for u in range(2)]

    barrier = pltpu.get_barrier_semaphore()

    def hello(to):
        pl.semaphore_signal(barrier, inc=1, device_id=to, device_id_type=MESH)

    def hello_other(to):
        @pl.when(jnp.logical_not(is_me(to)))
        def _():
            hello(to)

    for to in (right, left, sibling, partner):
        hello(to)
    for to in [a_from] + b_from + [result_from]:
        hello_other(to)

    @pl.when(jnp.logical_not(first))
    def _():
        hello(prev_from)

    def hello_all(s, carry):
        hello_other((s, owner_fsdp))
        return carry

    @pl.when(first)
    def _():
        lax.fori_loop(0, 16, hello_all, 0)

    def other(to):
        return jnp.where(is_me(to), 0, 1)

    own_share = jnp.where(owner_fsdp == fsdp, 15, 16)
    expected = 4 + other(in_to) + other(a_to) + other(b_to[0]) + other(b_to[1])
    pl.semaphore_wait(barrier, expected + jnp.where(last, own_share, 1))

    started = []

    def give(src, dst, send, recv, to):
        far = remote(src, dst, send, recv, to)
        near = pltpu.make_async_copy(src, dst, recv)

        @pl.when(is_me(to))
        def _():
            near.start()

        @pl.when(jnp.logical_not(is_me(to)))
        def _():
            far.start()

        started.append((is_me(to), far))

    give(wa_ref, w1.at[y, zlo // 2, zlo % 2], z_send.at[0], z_recv.at[0], a_to)
    for q in range(2):
        give(wb_ref, w2.at[y, zlo // 2, zlo % 2], z_send.at[1 + q], z_recv.at[1 + zlo % 2], b_to[q])
    give(in_ref, xin.at[:, pl.ds(2 * section, 2)], in_send.at[0], in_recv.at[0], in_to)
    give(seg_ref, segs.at[section], in_send.at[1], in_recv.at[1], in_to)

    sends = []

    def send(ref, sems, recv, to):
        copy = remote(ref, ref, sems.at[len([1 for kind, _ in sends if kind is sems])], recv, to)
        copy.start()
        sends.append((sems, copy))

    def ring(ref, direction, step, part):
        recv = ring_recv.at[(direction * 4 + step) * 3 + part]
        send(ref, ring_send, recv, right if direction == 0 else left)

    def cross(ref, column):
        send(ref, cross_send, cross_recv.at[column], partner)

    def across(ref, part):
        send(ref, sib_send, sib_recv.at[part], sibling)

    def column_of(direction, step):
        return (y + (8 - step if direction == 0 else step)) % 8

    def ring_last(column, direction):
        ref = w1.at[column, side, core]
        return remote(
            ref, ref, ring_send.at[15], ring_recv.at[(direction * 4 + 3) * 3],
            right if direction == 0 else left,
        )

    def w1_at(column):
        return w1.at[column, side, core]

    def w2_at(column, u):
        return w2.at[column, core, u]

    def w2_both(column):
        return w2.at[column, core]

    arrived(w1_at(y), z_recv.at[0])
    for direction in range(2):
        ring(w1_at(y), direction, 0, 0)
    cross(w1_at(y), y)
    across(w1_at(y), 0)
    for u in range(2):
        arrived(w2_at(y, u), z_recv.at[1 + u])
    for direction in range(2):
        ring(w2_both(y), direction, 0, 1)
    across(w2_both(y), 1)

    def crossed(column):
        ref = w1.at[column, 1 - side, core]
        arrived(ref, cross_recv.at[column])
        across(ref, 0)

    for step in range(1, 4):
        for direction in range(2):
            column = column_of(direction, step)
            arrived(w1_at(column), ring_recv.at[(direction * 4 + step - 1) * 3])
            if step < 3:
                ring(w1_at(column), direction, step, 0)
            else:
                @pl.when(core == direction)
                def _(column=column, direction=direction):
                    ring_last(column, direction).start()
            cross(w1_at(column), column)
            across(w1_at(column), 0)
        for direction in range(2):
            column = column_of(direction, step)
            arrived(w2_both(column), ring_recv.at[(direction * 4 + step - 1) * 3 + 1])
            ring(w2_both(column) if step < 3 else w2_at(column, direction), direction, step, 1)
            across(w2_both(column), 1)
        if step == 1:
            crossed(y)
        else:
            for direction in range(2):
                crossed(column_of(direction, step - 1))
    column = (y + 4) % 8
    for direction in range(2):
        @pl.when(core == direction)
        def _(direction=direction):
            arrived(w1_at(column), ring_recv.at[(direction * 4 + 3) * 3])
    cross(w1_at(column), column)
    across(w1_at(column), 0)
    for direction in range(2):
        arrived(w2_at(column, direction), ring_recv.at[(direction * 4 + 3) * 3 + 1])
        across(w2_at(column, direction), 1)
    for direction in range(2):
        crossed(column_of(direction, 3))
    crossed(column)
    arrived(w1.at[:, :, 1 - core], sib_recv.at[0])
    arrived(w2.at[:, 1 - core], sib_recv.at[1])

    def local(m, j):
        return pltpu.make_async_copy(xsend.at[m, j], xrecv.at[m, j], x_recv.at[m * CHUNKS + j])

    @pl.when(first)
    def _():
        arrived(xin, in_recv.at[0])
        arrived(segs, in_recv.at[1])
        row = lax.broadcasted_iota(jnp.int32, (SEQ, 128), 0)
        key = lax.broadcasted_iota(jnp.int32, (SEQ, 128), 1) % SEQ
        to = lax.broadcasted_iota(jnp.int32, (SEQ, SEQ), 0)
        source = lax.broadcasted_iota(jnp.int32, (SEQ, SEQ), 1)
        order = jnp.where(to == 2 * (source % 16) + source // 16, 1.0, 0.0).astype(BF16)

        def load(m, carry):
            wide[...] = xin[m].astype(F32)
            for i in range(16):
                xsend[m, i // 4, :, (i % 4) * 128 : (i % 4) * 128 + 128] = wide[:, i, :].astype(BF16)
            for j in range(CHUNKS):
                local(m, j).start()
            return carry

        lax.fori_loop(0, MICRO, load, 0)
        for m in range(MICRO):
            seg = jnp.concatenate([segs[:, 2 * m, :], segs[:, 2 * m + 1, :]], axis=0)
            seg = jnp.dot(order, seg.astype(BF16), preferred_element_type=F32)
            of_key = jnp.sum(jnp.where(row == key, seg, 0.0), axis=0, keepdims=True)
            allowed = (row >= key) & (seg == of_key)
            mask[m] = jnp.where(allowed, 1.0, 0.0).astype(BF16)

    @pl.when(jnp.logical_not(first))
    def _():
        arrived(mask, mask_recv)

    mask_copy = remote(mask, mask, mask_send, mask_recv, next_to)

    @pl.when(jnp.logical_not(last))
    def _():
        mask_copy.start()

    def hop(m, j):
        n = m * CHUNKS + j
        return remote(xsend.at[m, j], xrecv.at[m, j], x_send.at[n], x_recv.at[n], next_to)

    def delivery(m, s):
        return remote(
            staged.at[m, pl.ds(2 * s, 2)], owned.at[m], o_send.at[m * 16 + s], o_recv,
            (s, owner_fsdp),
        )

    def keep(m):
        return pltpu.make_async_copy(staged.at[m, pl.ds(2 * section, 2)], owned.at[m], o_recv)

    def one(m, carry):
        accs = [None] * 6
        squares = jnp.zeros((SEQ, 1), F32)
        for j in range(CHUNKS):
            arrived(xrecv.at[m, j], x_recv.at[m * CHUNKS + j])
            h = xrecv[m, j]
            hf = h.astype(F32)
            squares = squares + jnp.sum(hf * hf, axis=1, keepdims=True)
            for n in (4, 5, 0, 1, 2, 3):
                weight = w1[2 * j : 2 * j + 2, :, :, :, 256 * n : 256 * n + 256]
                term = jnp.dot(h, weight.reshape(CHUNK, 256), preferred_element_type=F32)
                accs[n] = term if accs[n] is None else accs[n] + term
        attended = attention(accs, squares, cos_ref[...], sin_ref[...], mask[m].astype(F32) > 0.5)
        for j in range(CHUNKS):
            weight = w2[:, :, :, :, j * CHUNK : (j + 1) * CHUNK].reshape(QW, CHUNK)
            update = jnp.dot(attended, weight, preferred_element_type=F32)
            h = xrecv[m, j].astype(F32) + update

            @pl.when(jnp.logical_not(last))
            def _(j=j, h=h):
                xsend[m, j] = h.astype(BF16)
                hop(m, j).start()

            @pl.when(last)
            def _(j=j, h=h):
                for i in range(4):
                    wide[:, 4 * j + i, :] = h[:, 128 * i : 128 * i + 128]

        @pl.when(last)
        def _():
            staged[m] = wide[...].astype(BF16)

            def hand(s, carry):
                mine = (s == section) & (owner_fsdp == fsdp)

                @pl.when(mine)
                def _():
                    keep(m).start()

                @pl.when(jnp.logical_not(mine))
                def _():
                    delivery(m, s).start()

                return carry

            lax.fori_loop(0, 16, hand, 0)

        return carry

    lax.fori_loop(0, MICRO, one, 0)

    arrived(owned, o_recv)
    out_ref[...] = owned[...]

    for mine, far in started:
        @pl.when(jnp.logical_not(mine))
        def _(far=far):
            far.wait_send()

    for _, copy in sends:
        copy.wait_send()
    for direction in range(2):
        @pl.when(core == direction)
        def _(direction=direction):
            ring_last(column_of(direction, 3), direction).wait_send()

    @pl.when(jnp.logical_not(last))
    def _():
        mask_copy.wait_send()

        def drain(n, carry):
            hop(n // CHUNKS, n % CHUNKS).wait_send()
            return carry

        lax.fori_loop(0, MICRO * CHUNKS, drain, 0)

    @pl.when(last)
    def _():
        def drain(n, carry):
            @pl.when(jnp.logical_not((n % 16 == section) & (owner_fsdp == fsdp)))
            def _():
                delivery(n // 16, n % 16).wait_send()

            return carry

        lax.fori_loop(0, MICRO * 16, drain, 0)


def shards(inputs, segments, norm_gains, w_query, w_keyval, w_output):
    positions = inputs[:, 0].reshape(MICRO, 2, 16, 128)
    segs = jnp.broadcast_to(segments[:, 0].reshape(MICRO * 2, 1), (MICRO * 2, 128)).astype(F32)
    gains = norm_gains[0].astype(F32)[:, None]
    wa = jnp.concatenate([w_query[0], w_keyval[0]], axis=1).astype(F32) * gains
    cosine, sine = rope_tables()
    vmem = pl.BlockSpec(memory_space=pltpu.VMEM)
    hbm = pl.BlockSpec(memory_space=pl.ANY)
    dma = pltpu.SemaphoreType.DMA
    out = pl.pallas_call(
        kernel,
        out_shape=jax.ShapeDtypeStruct((MICRO, 2, 16, 128), BF16),
        in_specs=[hbm, hbm, hbm, hbm, vmem, vmem],
        out_specs=vmem,
        scratch_shapes=[
            pltpu.VMEM((8, 2, 2, 64, QKV), BF16),
            pltpu.VMEM((8, 2, 2, 32, WIDTH), BF16),
            pltpu.VMEM((MICRO, SEQ, 16, 128), BF16),
            pltpu.VMEM((16, MICRO * 2, 128), F32),
            pltpu.VMEM((SEQ, 16, 128), F32),
            pltpu.VMEM((MICRO, SEQ, 128), BF16),
            pltpu.VMEM((MICRO, CHUNKS, SEQ, CHUNK), BF16),
            pltpu.VMEM((MICRO, CHUNKS, SEQ, CHUNK), BF16),
            pltpu.VMEM((MICRO, SEQ, 16, 128), BF16),
            pltpu.VMEM((MICRO, 2, 16, 128), BF16),
            dma((3,)), dma((3,)), dma((16,)), dma((24,)), dma((32,)), dma((2,)), dma((8,)), dma((8,)),
            dma((2,)), dma((2,)), dma, dma, dma((16,)), dma((16,)), dma((64,)), dma,
        ],
        compiler_params=pltpu.CompilerParams(
            collective_id=0, has_side_effects=True, vmem_limit_bytes=40 * 1024 * 1024
        ),
        name="stack",
    )(positions, segs, wa.astype(BF16), w_output[0], jnp.asarray(cosine), jnp.asarray(sine))
    return out.reshape(MICRO, 1, 2, WIDTH)


def solution(mesh):
    return jax.shard_map(
        shards,
        mesh=mesh,
        in_specs=(
            P(None, "fsdp", "section", None),
            P(None, "fsdp", "section"),
            P("section", "fsdp"),
            P("section", "fsdp", None),
            P("section", "fsdp", None),
            P("section", "fsdp", None),
        ),
        out_specs=P(None, "fsdp", "section", None),
        check_vma=False,
    )
```

time: 218 us -> 179 us (0.82)
  Pallas kernels: 214 us -> 174 us
    pallas_call x1, Pallas kernels: 214 us -> 174 us  [shards(): pl.pallas_call(kernel, out_shape=jax.ShapeDtypeStruct((MICRO, 2, 16, 128)...]
where the time goes in v2:
time: 179 us; the launch traced here: 178 us
  Pallas kernels  174 us (97%)
  other arithmetic  2.44 us (1%)
    pallas_call x1, Pallas kernels, shards(): pl.pallas_call(kernel, out_shape=jax.ShapeDtypeStruct((MICRO, 2, 16, 128)...  174 us

profile of v2, /device:TPU:1, one launch (start us, length us, event | category | flops | bytes accessed | tf_op | source)
XLA Modules:
  0.0 178.4 jit_solution(17886564822923171648)
XLA Ops:
  0.0 0.0 copy-start.3
  0.0 0.7 bitcast_convert_fusion
  0.7 0.7 convert_element_type.21
  1.4 0.1 copy.11
  1.5 0.1 convert_element_type.22
  1.6 0.1 broadcast_in_dim.2.seg_ref
  1.6 0.8 reshape_squeeze.4.in_ref
  2.4 0.0 copy-done.3
  2.4 0.0 copy-start
  2.4 0.0 copy-start.1
  2.4 0.0 copy-start.2
  2.5 1.1 multiply_convert_fusion.wa_ref
  3.5 0.0 copy-done
  3.5 0.0 copy-done.1
  3.6 0.0 copy-done.2
  3.6 174.2 %stack.1 = bf16[4,2,16,128]{3,2,1,0:T(8,128)(2,1)S(1)} custom-call(bf16[4,2,16,128]{3,2,1,0:T(8,128)(2,1)S(1)} %reshape_squeeze.4.in_ref, f32[8,128]{1,0:T(8,128)S(1)} %broadcast_in_dim.2.seg_ref, bf16[64,1536]{1,0:T(8,128)(2,1)S(1)} %multiply_convert_fusion.wa_ref, bf16[32,2048]{1,0:T(8,128)(2,1)S(1)} %bitcast.11, f32[32,128]{1,0:T(8,128)S(1)} %copy-done.2, ...), custom_call_target="tpu_custom_call" | custom-call | tf_op jit(solution)/shard_map/stack/pallas_call | solution.py:432
  177.7 0.6 reshape.12
Async XLA Ops:
  0.0 2.4 %copy-start.3 = (bf16[1,64,512]{2,1,0:T(8,128)(2,1)S(1)}, bf16[1,64,512]{2,1,0:T(8,128)(2,1)}, u32[]{:S(2)}) copy-start(bf16[1,64,512]{2,1,0:T(8,128)(2,1)} %param.12) | copy-start | bytes 196612
  2.4 1.1 copy-start
  2.4 1.1 copy-start.1
  2.4 1.1 copy-start.2

commit v3 on v2

--- a/solution.py
+++ b/solution.py
@@ -16,6 +16,7 @@
 WIDTH = 2048
 CHUNKS = 4
 CHUNK = WIDTH // CHUNKS
+TILES = CHUNK // 128
 QW = 1024
 KW = 256
 QKV = 1536
@@ -66,12 +67,10 @@
     exps = jnp.concatenate(exps, axis=0)
     most = (exps * 0.99609375).astype(BF16)
     rest = (exps - most.astype(F32)).astype(BF16)
-    row = lax.broadcasted_iota(jnp.int32, (128, 128), 0) // SEQ
-    col = lax.broadcasted_iota(jnp.int32, (128, 128), 1) // SEQ
+    row = lax.broadcasted_iota(jnp.int32, (256, 128), 0) % 128 // SEQ
+    col = lax.broadcasted_iota(jnp.int32, (256, 128), 1) // SEQ
     same = jnp.where(row == col, 1.0, 0.0).astype(BF16)
-    total = jnp.dot(most, same, preferred_element_type=F32) + jnp.dot(
-        rest, same, preferred_element_type=F32
-    )
+    total = jnp.dot(jnp.concatenate([most, rest], axis=1), same, preferred_element_type=F32)
     power = jnp.where(total > 1.0, 2.0**-8, 2.0**8)
     probs = (exps * power) * (1.0 / (total * power))
     outs = []
@@ -94,7 +93,7 @@
     y, zlo = fsdp // 4, fsdp % 4
     z = zhi * 4 + zlo
     side = ((x + 1) // 2) % 2
-    layer = jnp.where(x < 2, (z + 6) % 8, 8 + (9 - z) % 8)
+    layer = jnp.where(x < 2, (z + 7) % 8, 8 + (8 - z) % 8)
     first, last = layer == 0, layer == LAST
     plane = section - core
 
@@ -104,7 +103,7 @@
     def host(of_layer, of_side, at_core):
         early = of_layer < 8
         at_x = jnp.where(early, of_side, 3 - of_side)
-        return place(at_x, jnp.where(early, of_layer + 2, 17 - of_layer) % 8, at_core)
+        return place(at_x, jnp.where(early, of_layer + 1, 16 - of_layer) % 8, at_core)
 
     def remote(src, dst, send, recv, to):
         return pltpu.make_async_remote_copy(
@@ -146,6 +145,7 @@
 
     for to in (right, left, sibling, partner):
         hello(to)
+
     for to in [a_from] + b_from + [result_from]:
         hello_other(to)
 
@@ -168,27 +168,34 @@
     expected = 4 + other(in_to) + other(a_to) + other(b_to[0]) + other(b_to[1])
     pl.semaphore_wait(barrier, expected + jnp.where(last, own_share, 1))
 
-    started = []
-
     def give(src, dst, send, recv, to):
-        far = remote(src, dst, send, recv, to)
-        near = pltpu.make_async_copy(src, dst, recv)
-
         @pl.when(is_me(to))
         def _():
-            near.start()
+            pltpu.make_async_copy(src, dst, recv).start()
 
         @pl.when(jnp.logical_not(is_me(to)))
         def _():
-            far.start()
-
-        started.append((is_me(to), far))
-
-    give(wa_ref, w1.at[y, zlo // 2, zlo % 2], z_send.at[0], z_recv.at[0], a_to)
-    for q in range(2):
-        give(wb_ref, w2.at[y, zlo // 2, zlo % 2], z_send.at[1 + q], z_recv.at[1 + zlo % 2], b_to[q])
-    give(in_ref, xin.at[:, pl.ds(2 * section, 2)], in_send.at[0], in_recv.at[0], in_to)
-    give(seg_ref, segs.at[section], in_send.at[1], in_recv.at[1], in_to)
+            remote(src, dst, send, recv, to).start()
+
+    def given(src, dst, send, recv, to):
+        @pl.when(jnp.logical_not(is_me(to)))
+        def _():
+            remote(src, dst, send, recv, to).wait_send()
+
+    own_a = (wa_ref, w1.at[y, zlo // 2, zlo % 2], z_send.at[0], z_recv.at[0], a_to)
+    own_b = [
+        (wb_ref, w2.at[y, zlo // 2, zlo % 2], z_send.at[1 + q], z_recv.at[1 + zlo % 2], b_to[q])
+        for q in range(2)
+    ]
+    own_in = [
+        (in_ref, xin.at[:, pl.ds(2 * section, 2)], in_send.at[0], in_recv.at[0], in_to),
+        (seg_ref, segs.at[section], in_send.at[1], in_recv.at[1], in_to),
+    ]
+
+    give(*own_a)
+    given(*own_a)
+    for copy in own_in + own_b:
+        give(*copy)
 
     sends = []
 
@@ -264,22 +271,6 @@
         else:
             for direction in range(2):
                 crossed(column_of(direction, step - 1))
-    column = (y + 4) % 8
-    for direction in range(2):
-        @pl.when(core == direction)
-        def _(direction=direction):
-            arrived(w1_at(column), ring_recv.at[(direction * 4 + 3) * 3])
-    cross(w1_at(column), column)
-    across(w1_at(column), 0)
-    for direction in range(2):
-        arrived(w2_at(column, direction), ring_recv.at[(direction * 4 + 3) * 3 + 1])
-        across(w2_at(column, direction), 1)
-    for direction in range(2):
-        crossed(column_of(direction, 3))
-    crossed(column)
-    arrived(w1.at[:, :, 1 - core], sib_recv.at[0])
-    arrived(w2.at[:, 1 - core], sib_recv.at[1])
-
     def local(m, j):
         return pltpu.make_async_copy(xsend.at[m, j], xrecv.at[m, j], x_recv.at[m * CHUNKS + j])
 
@@ -296,7 +287,7 @@
         def load(m, carry):
             wide[...] = xin[m].astype(F32)
             for i in range(16):
-                xsend[m, i // 4, :, (i % 4) * 128 : (i % 4) * 128 + 128] = wide[:, i, :].astype(BF16)
+                xsend[m, i // TILES, :, (i % TILES) * 128 : (i % TILES) * 128 + 128] = wide[:, i, :].astype(BF16)
             for j in range(CHUNKS):
                 local(m, j).start()
             return carry
@@ -309,6 +300,22 @@
             allowed = (row >= key) & (seg == of_key)
             mask[m] = jnp.where(allowed, 1.0, 0.0).astype(BF16)
 
+    column = (y + 4) % 8
+    for direction in range(2):
+        @pl.when(core == direction)
+        def _(direction=direction):
+            arrived(w1_at(column), ring_recv.at[(direction * 4 + 3) * 3])
+    cross(w1_at(column), column)
+    across(w1_at(column), 0)
+    for direction in range(2):
+        arrived(w2_at(column, direction), ring_recv.at[(direction * 4 + 3) * 3 + 1])
+        across(w2_at(column, direction), 1)
+    for direction in range(2):
+        crossed(column_of(direction, 3))
+    crossed(column)
+    arrived(w1.at[:, :, 1 - core], sib_recv.at[0])
+    arrived(w2.at[:, 1 - core], sib_recv.at[1])
+
     @pl.when(jnp.logical_not(first))
     def _():
         arrived(mask, mask_recv)
@@ -332,16 +339,17 @@
     def keep(m):
         return pltpu.make_async_copy(staged.at[m, pl.ds(2 * section, 2)], owned.at[m], o_recv)
 
-    def one(m, carry):
+    def one(m, final):
         accs = [None] * 6
         squares = jnp.zeros((SEQ, 1), F32)
+        span = 8 // CHUNKS
         for j in range(CHUNKS):
             arrived(xrecv.at[m, j], x_recv.at[m * CHUNKS + j])
             h = xrecv[m, j]
             hf = h.astype(F32)
             squares = squares + jnp.sum(hf * hf, axis=1, keepdims=True)
             for n in (4, 5, 0, 1, 2, 3):
-                weight = w1[2 * j : 2 * j + 2, :, :, :, 256 * n : 256 * n + 256]
+                weight = w1[span * j : span * (j + 1), :, :, :, 256 * n : 256 * n + 256]
                 term = jnp.dot(h, weight.reshape(CHUNK, 256), preferred_element_type=F32)
                 accs[n] = term if accs[n] is None else accs[n] + term
         attended = attention(accs, squares, cos_ref[...], sin_ref[...], mask[m].astype(F32) > 0.5)
@@ -349,19 +357,14 @@
             weight = w2[:, :, :, :, j * CHUNK : (j + 1) * CHUNK].reshape(QW, CHUNK)
             update = jnp.dot(attended, weight, preferred_element_type=F32)
             h = xrecv[m, j].astype(F32) + update
-
-            @pl.when(jnp.logical_not(last))
-            def _(j=j, h=h):
+            if final:
+                for i in range(TILES):
+                    wide[:, TILES * j + i, :] = h[:, 128 * i : 128 * i + 128]
+            else:
                 xsend[m, j] = h.astype(BF16)
                 hop(m, j).start()
 
-            @pl.when(last)
-            def _(j=j, h=h):
-                for i in range(4):
-                    wide[:, 4 * j + i, :] = h[:, 128 * i : 128 * i + 128]
-
-        @pl.when(last)
-        def _():
+        if final:
             staged[m] = wide[...].astype(BF16)
 
             def hand(s, carry):
@@ -379,18 +382,26 @@
 
             lax.fori_loop(0, 16, hand, 0)
 
-        return carry
-
-    lax.fori_loop(0, MICRO, one, 0)
+    def run(final):
+        def step(m, carry):
+            one(m, final)
+            return carry
+
+        lax.fori_loop(0, MICRO, step, 0)
+
+    @pl.when(last)
+    def _():
+        run(True)
+
+    @pl.when(jnp.logical_not(last))
+    def _():
+        run(False)
 
     arrived(owned, o_recv)
     out_ref[...] = owned[...]
 
-    for mine, far in started:
-        @pl.when(jnp.logical_not(mine))
-        def _(far=far):
-            far.wait_send()
-
+    for copy in own_b + own_in:
+        given(*copy)
     for _, copy in sends:
         copy.wait_send()
     for direction in range(2):
@@ -429,6 +440,7 @@
     vmem = pl.BlockSpec(memory_space=pltpu.VMEM)
     hbm = pl.BlockSpec(memory_space=pl.ANY)
     dma = pltpu.SemaphoreType.DMA
+    hops = MICRO * CHUNKS
     out = pl.pallas_call(
         kernel,
         out_shape=jax.ShapeDtypeStruct((MICRO, 2, 16, 128), BF16),
@@ -446,7 +458,7 @@
             pltpu.VMEM((MICRO, SEQ, 16, 128), BF16),
             pltpu.VMEM((MICRO, 2, 16, 128), BF16),
             dma((3,)), dma((3,)), dma((16,)), dma((24,)), dma((32,)), dma((2,)), dma((8,)), dma((8,)),
-            dma((2,)), dma((2,)), dma, dma, dma((16,)), dma((16,)), dma((64,)), dma,
+            dma((2,)), dma((2,)), dma, dma, dma((hops,)), dma((hops,)), dma((64,)), dma,
         ],
         compiler_params=pltpu.CompilerParams(
             collective_id=0, has_side_effects=True, vmem_limit_bytes=40 * 1024 * 1024

time: 179 us -> 175 us (0.978)
  Pallas kernels: 174 us -> 170 us
    pallas_call x1, Pallas kernels: 174 us -> 170 us  [shards(): pl.pallas_call(kernel, out_shape=jax.ShapeDtypeStruct((MICRO, 2, 16, 128)...]
where the time goes in v3:
time: 175 us; the launch traced here: 174 us
  Pallas kernels  170 us (97%)
  other arithmetic  2.44 us (1%)
    pallas_call x1, Pallas kernels, shards(): pl.pallas_call(kernel, out_shape=jax.ShapeDtypeStruct((MICRO, 2, 16, 128)...  170 us

profile of v3, /device:TPU:1, one launch (start us, length us, event | category | flops | bytes accessed | tf_op | source)
XLA Modules:
  0.0 173.9 jit_solution(3848277837930462302)
XLA Ops:
  0.0 0.0 copy-start.3
  0.0 0.7 bitcast_convert_fusion
  0.7 0.7 convert_element_type.21
  1.4 0.1 copy.11
  1.5 0.1 convert_element_type.22
  1.6 0.1 broadcast_in_dim.2.seg_ref
  1.6 0.8 reshape_squeeze.4.in_ref
  2.4 0.0 copy-done.3
  2.4 0.0 copy-start
  2.4 0.0 copy-start.1
  2.4 0.0 copy-start.2
  2.5 1.1 multiply_convert_fusion.wa_ref
  3.5 0.0 copy-done
  3.5 0.0 copy-done.1
  3.6 0.0 copy-done.2
  3.6 169.7 %stack.1 = bf16[4,2,16,128]{3,2,1,0:T(8,128)(2,1)S(1)} custom-call(bf16[4,2,16,128]{3,2,1,0:T(8,128)(2,1)S(1)} %reshape_squeeze.4.in_ref, f32[8,128]{1,0:T(8,128)S(1)} %broadcast_in_dim.2.seg_ref, bf16[64,1536]{1,0:T(8,128)(2,1)S(1)} %multiply_convert_fusion.wa_ref, bf16[32,2048]{1,0:T(8,128)(2,1)S(1)} %bitcast.11, f32[32,128]{1,0:T(8,128)S(1)} %copy-done.2, ...), custom_call_target="tpu_custom_call" | custom-call | tf_op jit(solution)/shard_map/stack/pallas_call | solution.py:444
  173.2 0.6 reshape.12
Async XLA Ops:
  0.0 2.4 %copy-start.3 = (bf16[1,64,512]{2,1,0:T(8,128)(2,1)S(1)}, bf16[1,64,512]{2,1,0:T(8,128)(2,1)}, u32[]{:S(2)}) copy-start(bf16[1,64,512]{2,1,0:T(8,128)(2,1)} %param.12) | copy-start | bytes 196612
  2.4 1.1 copy-start
  2.4 1.1 copy-start.1
  2.4 1.1 copy-start.2

commit v4 on v3

--- a/solution.py
+++ b/solution.py
@@ -83,8 +83,8 @@
 
 
 def kernel(
-    in_ref, seg_ref, wa_ref, wb_ref, cos_ref, sin_ref, out_ref,
-    w1, w2, xin, segs, wide, mask, xrecv, xsend, staged, owned,
+    rows_ref, ids_ref, gain_ref, wq_ref, wkv_ref, wo_ref, table_ref, out_ref,
+    raw_q, raw_kv, raw_o, tables, wa_ref, tall, in_ref, seg_ref, raw_sem, w1, w2, xin, segs, wide, mask, xrecv, xsend, staged, owned,
     z_send, z_recv, ring_send, ring_recv, sib_send, sib_recv, cross_send, cross_recv,
     in_send, in_recv, mask_send, mask_recv, x_send, x_recv, o_send, o_recv,
 ):
@@ -125,7 +125,7 @@
     in_to = host(jnp.int32(0), zlo // 2, zlo % 2)
     own_layer = section
     a_to = host(own_layer, zlo // 2, zlo % 2)
-    b_to = [host(own_layer, q, zlo // 2) for q in range(2)]
+    b_to = host(own_layer, zlo // 2, zlo // 2)
     next_to = host(jnp.minimum(layer + 1, LAST), side, core)
     prev_from = host(jnp.maximum(layer - 1, 0), side, core)
     owner_fsdp = y * 4 + 2 * side + core
@@ -133,6 +133,18 @@
     a_from = (layer, y * 4 + 2 * side + core)
     b_from = [(layer, y * 4 + 2 * core + u) for u in range(2)]
 
+    raws = [
+        pltpu.make_async_copy(src, dst, raw_sem.at[n])
+        for n, (src, dst) in enumerate(
+            (
+                (wq_ref.at[0], raw_q), (wkv_ref.at[0], raw_kv), (wo_ref.at[0], raw_o),
+                (table_ref, tables),
+            )
+        )
+    ]
+    for raw in raws:
+        raw.start()
+
     barrier = pltpu.get_barrier_semaphore()
 
     def hello(to):
@@ -146,8 +158,13 @@
     for to in (right, left, sibling, partner):
         hello(to)
 
-    for to in [a_from] + b_from + [result_from]:
+    for to in (a_from, result_from):
         hello_other(to)
+
+    @pl.when(core == side)
+    def _():
+        for to in b_from:
+            hello_other(to)
 
     @pl.when(jnp.logical_not(first))
     def _():
@@ -164,8 +181,27 @@
     def other(to):
         return jnp.where(is_me(to), 0, 1)
 
+    row = lax.broadcasted_iota(jnp.int32, (64, 64), 0)
+    col = lax.broadcasted_iota(jnp.int32, (64, 64), 1)
+    gains = jnp.sum(
+        jnp.where(row == col, gain_ref[...].astype(F32), 0.0), axis=1, keepdims=True
+    )
+    for i in range(16):
+        tall[:, :, i, :] = rows_ref[:, 0, :, 128 * i : 128 * i + 128].astype(F32)
+    in_ref[...] = tall[...].astype(BF16)
+    row = lax.broadcasted_iota(jnp.int32, (MICRO * 2, 128), 0)
+    ids = jnp.zeros((MICRO * 2, 128), jnp.int32)
+    for m in range(MICRO):
+        for p in range(2):
+            ids = jnp.where(row == 2 * m + p, ids_ref[0, p, m], ids)
+    seg_ref[...] = ids.astype(F32)
+    for raw in raws:
+        raw.wait()
+    wa_ref[:, :QW] = (raw_q[...].astype(F32) * gains).astype(BF16)
+    wa_ref[:, QW:] = (raw_kv[...].astype(F32) * gains).astype(BF16)
+
     own_share = jnp.where(owner_fsdp == fsdp, 15, 16)
-    expected = 4 + other(in_to) + other(a_to) + other(b_to[0]) + other(b_to[1])
+    expected = 4 + other(in_to) + other(a_to) + other(b_to)
     pl.semaphore_wait(barrier, expected + jnp.where(last, own_share, 1))
 
     def give(src, dst, send, recv, to):
@@ -183,10 +219,7 @@
             remote(src, dst, send, recv, to).wait_send()
 
     own_a = (wa_ref, w1.at[y, zlo // 2, zlo % 2], z_send.at[0], z_recv.at[0], a_to)
-    own_b = [
-        (wb_ref, w2.at[y, zlo // 2, zlo % 2], z_send.at[1 + q], z_recv.at[1 + zlo % 2], b_to[q])
-        for q in range(2)
-    ]
+    own_b = (raw_o, w2.at[y, zlo // 2, zlo % 2], z_send.at[1], z_recv.at[1 + zlo % 2], b_to)
     own_in = [
         (in_ref, xin.at[:, pl.ds(2 * section, 2)], in_send.at[0], in_recv.at[0], in_to),
         (seg_ref, segs.at[section], in_send.at[1], in_recv.at[1], in_to),
@@ -194,7 +227,7 @@
 
     give(*own_a)
     given(*own_a)
-    for copy in own_in + own_b:
+    for copy in own_in + [own_b]:
         give(*copy)
 
     sends = []
@@ -238,8 +271,18 @@
         ring(w1_at(y), direction, 0, 0)
     cross(w1_at(y), y)
     across(w1_at(y), 0)
-    for u in range(2):
-        arrived(w2_at(y, u), z_recv.at[1 + u])
+    column_b = remote(w2_both(y), w2_both(y), z_send.at[2], z_recv.at[3], partner)
+
+    @pl.when(core == side)
+    def _():
+        for u in range(2):
+            arrived(w2_at(y, u), z_recv.at[1 + u])
+        column_b.start()
+
+    @pl.when(core != side)
+    def _():
+        arrived(w2_both(y), z_recv.at[3])
+
     for direction in range(2):
         ring(w2_both(y), direction, 0, 1)
     across(w2_both(y), 1)
@@ -352,7 +395,7 @@
                 weight = w1[span * j : span * (j + 1), :, :, :, 256 * n : 256 * n + 256]
                 term = jnp.dot(h, weight.reshape(CHUNK, 256), preferred_element_type=F32)
                 accs[n] = term if accs[n] is None else accs[n] + term
-        attended = attention(accs, squares, cos_ref[...], sin_ref[...], mask[m].astype(F32) > 0.5)
+        attended = attention(accs, squares, tables[0], tables[1], mask[m].astype(F32) > 0.5)
         for j in range(CHUNKS):
             weight = w2[:, :, :, :, j * CHUNK : (j + 1) * CHUNK].reshape(QW, CHUNK)
             update = jnp.dot(attended, weight, preferred_element_type=F32)
@@ -400,8 +443,13 @@
     arrived(owned, o_recv)
     out_ref[...] = owned[...]
 
-    for copy in own_b + own_in:
+    for copy in own_in + [own_b]:
         given(*copy)
+
+    @pl.when(core == side)
+    def _():
+        column_b.wait_send()
+
     for _, copy in sends:
         copy.wait_send()
     for direction in range(2):
@@ -432,21 +480,26 @@
 
 
 def shards(inputs, segments, norm_gains, w_query, w_keyval, w_output):
-    positions = inputs[:, 0].reshape(MICRO, 2, 16, 128)
-    segs = jnp.broadcast_to(segments[:, 0].reshape(MICRO * 2, 1), (MICRO * 2, 128)).astype(F32)
-    gains = norm_gains[0].astype(F32)[:, None]
-    wa = jnp.concatenate([w_query[0], w_keyval[0]], axis=1).astype(F32) * gains
-    cosine, sine = rope_tables()
     vmem = pl.BlockSpec(memory_space=pltpu.VMEM)
-    hbm = pl.BlockSpec(memory_space=pl.ANY)
+    hbm = pl.BlockSpec(memory_space=pltpu.HBM)
+    smem = pl.BlockSpec(memory_space=pltpu.SMEM)
     dma = pltpu.SemaphoreType.DMA
     hops = MICRO * CHUNKS
     out = pl.pallas_call(
         kernel,
         out_shape=jax.ShapeDtypeStruct((MICRO, 2, 16, 128), BF16),
-        in_specs=[hbm, hbm, hbm, hbm, vmem, vmem],
+        in_specs=[vmem, smem, vmem, hbm, hbm, hbm, hbm],
         out_specs=vmem,
         scratch_shapes=[
+            pltpu.VMEM((64, QW), BF16),
+            pltpu.VMEM((64, QKV - QW), BF16),
+            pltpu.VMEM((32, WIDTH), BF16),
+            pltpu.VMEM((2, SEQ, 128), F32),
+            pltpu.VMEM((64, QKV), BF16),
+            pltpu.VMEM((MICRO, 2, 16, 128), F32),
+            pltpu.VMEM((MICRO, 2, 16, 128), BF16),
+            pltpu.VMEM((MICRO * 2, 128), F32),
+            dma((4,)),
             pltpu.VMEM((8, 2, 2, 64, QKV), BF16),
             pltpu.VMEM((8, 2, 2, 32, WIDTH), BF16),
             pltpu.VMEM((MICRO, SEQ, 16, 128), BF16),
@@ -457,14 +510,17 @@
             pltpu.VMEM((MICRO, CHUNKS, SEQ, CHUNK), BF16),
             pltpu.VMEM((MICRO, SEQ, 16, 128), BF16),
             pltpu.VMEM((MICRO, 2, 16, 128), BF16),
-            dma((3,)), dma((3,)), dma((16,)), dma((24,)), dma((32,)), dma((2,)), dma((8,)), dma((8,)),
+            dma((3,)), dma((4,)), dma((16,)), dma((24,)), dma((32,)), dma((2,)), dma((8,)), dma((8,)),
             dma((2,)), dma((2,)), dma, dma, dma((hops,)), dma((hops,)), dma((64,)), dma,
         ],
         compiler_params=pltpu.CompilerParams(
-            collective_id=0, has_side_effects=True, vmem_limit_bytes=40 * 1024 * 1024
+            collective_id=0, has_side_effects=True, vmem_limit_bytes=63 * 1024 * 1024
         ),
         name="stack",
-    )(positions, segs, wa.astype(BF16), w_output[0], jnp.asarray(cosine), jnp.asarray(sine))
+    )(
+        inputs, jnp.transpose(segments, (1, 2, 0)), norm_gains, w_query, w_keyval, w_output,
+        jnp.asarray(np.stack(rope_tables())),
+    )
     return out.reshape(MICRO, 1, 2, WIDTH)
 
 

time: 175 us -> 171 us (0.977)
  other arithmetic: 2.44 us -> 0 us
    convert_element_type x3 -> x0, other arithmetic: 2.44 us -> none  [the longest x1 1.07 us: shards(): wa.astype(BF16)]
where the time goes in v4:
time: 171 us
  Pallas kernels  169 us (99%)
    pallas_call x1, Pallas kernels, shards(): pl.pallas_call(kernel, out_shape=jax.ShapeDtypeStruct((MICRO, 2, 16, 128)...  169 us

profile of v4, /device:TPU:1, one launch (start us, length us, event | category | flops | bytes accessed | tf_op | source)
XLA Modules:
  0.0 170.6 jit_solution(2792382824463021058)
XLA Ops:
  0.0 169.3 %stack.1 = bf16[4,2,16,128]{3,2,1,0:T(8,128)(2,1)} custom-call(bf16[4,1,2,2048]{3,2,1,0:T(2,128)(2,1)} %rows_ref.1, s32[1,2,4]{2,1,0:T(2,128)} %bitcast.4, bf16[1,64]{1,0:T(2,128)(2,1)} %gain_ref.1, bf16[1,64,1024]{2,1,0:T(8,128)(2,1)} %wq_ref.1, bf16[1,64,512]{2,1,0:T(8,128)(2,1)} %wkv_ref.1, bf16[1,32,2048]{2,1,0:T(8,128)(2,1)} %wo_ref.1, ...), custom_call_target="tpu_custom_call" | custom-call | tf_op jit(solution)/shard_map/stack/pallas_call | solution.py:488
  169.3 1.4 reshape.3

commit v5 on v4

--- a/solution.py
+++ b/solution.py
@@ -226,8 +226,7 @@
     ]
 
     give(*own_a)
-    given(*own_a)
-    for copy in own_in + [own_b]:
+    for copy in [own_b] + own_in:
         give(*copy)
 
     sends = []
@@ -309,11 +308,6 @@
             arrived(w2_both(column), ring_recv.at[(direction * 4 + step - 1) * 3 + 1])
             ring(w2_both(column) if step < 3 else w2_at(column, direction), direction, step, 1)
             across(w2_both(column), 1)
-        if step == 1:
-            crossed(y)
-        else:
-            for direction in range(2):
-                crossed(column_of(direction, step - 1))
     def local(m, j):
         return pltpu.make_async_copy(xsend.at[m, j], xrecv.at[m, j], x_recv.at[m * CHUNKS + j])
 
@@ -353,8 +347,10 @@
     for direction in range(2):
         arrived(w2_at(column, direction), ring_recv.at[(direction * 4 + 3) * 3 + 1])
         across(w2_at(column, direction), 1)
-    for direction in range(2):
-        crossed(column_of(direction, 3))
+    crossed(y)
+    for step in range(1, 4):
+        for direction in range(2):
+            crossed(column_of(direction, step))
     crossed(column)
     arrived(w1.at[:, :, 1 - core], sib_recv.at[0])
     arrived(w2.at[:, 1 - core], sib_recv.at[1])
@@ -443,7 +439,7 @@
     arrived(owned, o_recv)
     out_ref[...] = owned[...]
 
-    for copy in own_in + [own_b]:
+    for copy in own_in + [own_a, own_b]:
         given(*copy)
 
     @pl.when(core == side)

time: 171 us -> 169 us (0.988)
  no operation moved by 1% of the time
where the time goes in v5:
time: 169 us
  Pallas kernels  168 us (99%)
    pallas_call x1, Pallas kernels, shards(): pl.pallas_call(kernel, out_shape=jax.ShapeDtypeStruct((MICRO, 2, 16, 128)...  168 us

profile of v5, /device:TPU:1, one launch (start us, length us, event | category | flops | bytes accessed | tf_op | source)
XLA Modules:
  0.0 169.0 jit_solution(702053405524231306)
XLA Ops:
  0.0 167.6 %stack.1 = bf16[4,2,16,128]{3,2,1,0:T(8,128)(2,1)} custom-call(bf16[4,1,2,2048]{3,2,1,0:T(2,128)(2,1)} %rows_ref.1, s32[1,2,4]{2,1,0:T(2,128)} %bitcast.4, bf16[1,64]{1,0:T(2,128)(2,1)} %gain_ref.1, bf16[1,64,1024]{2,1,0:T(8,128)(2,1)} %wq_ref.1, bf16[1,64,512]{2,1,0:T(8,128)(2,1)} %wkv_ref.1, bf16[1,32,2048]{2,1,0:T(8,128)(2,1)} %wo_ref.1, ...), custom_call_target="tpu_custom_call" | custom-call | tf_op jit(solution)/shard_map/stack/pallas_call | solution.py:484
  167.6 1.4 reshape.3

commit v6 on v5

--- a/solution.py
+++ b/solution.py
@@ -311,8 +311,7 @@
     def local(m, j):
         return pltpu.make_async_copy(xsend.at[m, j], xrecv.at[m, j], x_recv.at[m * CHUNKS + j])
 
-    @pl.when(first)
-    def _():
+    def load_all():
         arrived(xin, in_recv.at[0])
         arrived(segs, in_recv.at[1])
         row = lax.broadcasted_iota(jnp.int32, (SEQ, 128), 0)
@@ -336,6 +335,10 @@
             of_key = jnp.sum(jnp.where(row == key, seg, 0.0), axis=0, keepdims=True)
             allowed = (row >= key) & (seg == of_key)
             mask[m] = jnp.where(allowed, 1.0, 0.0).astype(BF16)
+
+    @pl.when(first & (core == 0))
+    def _():
+        load_all()
 
     column = (y + 4) % 8
     for direction in range(2):
@@ -354,6 +357,10 @@
     crossed(column)
     arrived(w1.at[:, :, 1 - core], sib_recv.at[0])
     arrived(w2.at[:, 1 - core], sib_recv.at[1])
+
+    @pl.when(first & (core == 1))
+    def _():
+        load_all()
 
     @pl.when(jnp.logical_not(first))
     def _():
@@ -406,20 +413,16 @@
         if final:
             staged[m] = wide[...].astype(BF16)
 
-            def hand(s, carry):
-                mine = (s == section) & (owner_fsdp == fsdp)
+            for s in range(16):
+                mine = (section == s) & (owner_fsdp == fsdp)
 
                 @pl.when(mine)
                 def _():
                     keep(m).start()
 
                 @pl.when(jnp.logical_not(mine))
-                def _():
+                def _(s=s):
                     delivery(m, s).start()
-
-                return carry
-
-            lax.fori_loop(0, 16, hand, 0)
 
     def run(final):
         def step(m, carry):

time: 169 us -> 169 us (level)
  no operation moved by 1% of the time
where the time goes in v6:
time: 169 us
  Pallas kernels  167 us (99%)
    pallas_call x1, Pallas kernels, shards(): pl.pallas_call(kernel, out_shape=jax.ShapeDtypeStruct((MICRO, 2, 16, 128)...  167 us

profile of v6, /device:TPU:1, one launch (start us, length us, event | category | flops | bytes accessed | tf_op | source)
XLA Modules:
  0.0 168.6 jit_solution(14529933515467749569)
XLA Ops:
  0.0 167.2 %stack.1 = bf16[4,2,16,128]{3,2,1,0:T(8,128)(2,1)} custom-call(bf16[4,1,2,2048]{3,2,1,0:T(2,128)(2,1)} %rows_ref.1, s32[1,2,4]{2,1,0:T(2,128)} %bitcast.4, bf16[1,64]{1,0:T(2,128)(2,1)} %gain_ref.1, bf16[1,64,1024]{2,1,0:T(8,128)(2,1)} %wq_ref.1, bf16[1,64,512]{2,1,0:T(8,128)(2,1)} %wkv_ref.1, bf16[1,32,2048]{2,1,0:T(8,128)(2,1)} %wo_ref.1, ...), custom_call_target="tpu_custom_call" | custom-call | tf_op jit(solution)/shard_map/stack/pallas_call | solution.py:487
  167.2 1.4 reshape.3
